TPU v7x, 32 devices: a whole 2x2x4 slice. The times are simulated.
32 devices in a mesh: dp: 8 (over y, x, core), pipe: 4 (over z).
Axes of the slice: x: 2, y: 2, z: 4, core: 2. Of those that a mesh axis runs over, the one named last changes fastest.
Arguments:
- stashed: bfloat16 [4, 4, 256, 8192], P('pipe', None, 'dp'), may hold values from -6 to 6
- kv_grads: bfloat16 [4, 4, 256, 2048], P('pipe', None, 'dp'), may hold values from -0.1875 to 0.1875
- branch_grads: bfloat16 [4, 256, 8192], P('pipe', 'dp'), may hold values from -6 to 6
- flora_seeds: int32 [4, 2], P('pipe'), may hold values from 0 to 99999
- plan: int32 [4, 4], P('pipe'), may hold values from 0 to 3, each once within a row
Outputs:
- compressed: float32 [4, 256, 2048], P('pipe')
- section_grads: bfloat16 [4, 256, 8192], P('pipe', 'dp')
Inputs may be any that keep to these rules, and one draw needn't show every extreme that they name: `plan`: each row is a permutation of the micro-batch numbers 0 to 3.
All inputs are finite; a program needn't handle non-finite values.
Results may differ from a plain program's by a relative error of at most 0.0051.
Values may be sent and summed in bfloat16 or wider, within the bound.
No kernel may reach another device: no remote copies, remote signals or barrier semaphores. Data moves between devices by JAX's collectives and lax.ppermute only.
A program may use at most 64 MiB of HBM per device.

v0:
```python
import math

import jax
import jax.numpy as jnp
from jax import lax
from jax.sharding import PartitionSpec as P

R = 256


def entering(value, axis, combine, identity):
    size, mine = (lax.axis_size(axis), lax.axis_index(axis))
    everything = lax.all_gather(value, axis)
    start = jnp.broadcast_to(jnp.asarray(identity, value.dtype), value.shape)

    def hop(k, before):
        at = size - 1 - k
        reached = at > mine
        new = combine(before, everything[at])
        return jnp.where(reached, new, before)

    return lax.fori_loop(0, size, hop, start)


def projection(seed_value, row_count, col_count):
    row_index = jnp.arange(row_count, dtype=jnp.int32)[:, None]
    col_index = jnp.arange(col_count, dtype=jnp.int32)[None, :]
    hashed_one = (row_index * 1031 + col_index * 2053 + seed_value * 3 + 7) % 32749
    hashed_two = (hashed_one * hashed_one + row_index * 17 + 5) % 32749
    hashed_three = (hashed_two * hashed_two + col_index * 29 + seed_value) % 32749
    scaled = hashed_three.astype(jnp.float32) * (2.0 / 32748.0) - 1.0
    return (scaled * math.sqrt(3.0 / row_count)).astype(jnp.bfloat16)


def contract(left_side, targets):
    return lax.dot_general(
        left_side, targets, (((0,), (0,)), ((), ())), preferred_element_type=jnp.float32
    )


def combine(earlier, later_part):
    return (earlier.astype(jnp.float32) + later_part.astype(jnp.float32)).astype(jnp.bfloat16)


def per_device(stashed, kv_grads, branch_grads, flora_seeds, plan):
    slot_count = stashed.shape[1]
    tokens_dev = stashed.shape[2]
    width_model = stashed.shape[3]
    kv_width = kv_grads.shape[3] // 2
    inputs = stashed[0].reshape(slot_count * tokens_dev, width_model)
    paired = jnp.take(kv_grads[0], plan[0], axis=0).reshape(slot_count * tokens_dev, 2 * kv_width)
    key_proj = projection(flora_seeds[0, 0], width_model, R)
    value_proj = projection(flora_seeds[0, 1], width_model, R)
    stacked_proj = jnp.concatenate([key_proj, value_proj], axis=1)
    projected = jnp.dot(inputs, stacked_proj, preferred_element_type=jnp.float32).astype(
        jnp.bfloat16
    )
    key_total = contract(projected[:, :R], paired[:, :kv_width])
    value_total = contract(projected[:, R:], paired[:, kv_width:])
    key_total, value_total = lax.psum((key_total, value_total), "dp")
    compressed = jnp.concatenate([key_total, value_total], axis=1)[None]
    own_branch = branch_grads[0]
    from_above = entering(own_branch, "pipe", combine, jnp.zeros_like(own_branch))
    running = combine(from_above, own_branch)
    return (compressed, running[None])


def solution(mesh):
    placed = (
        P("pipe", None, "dp", None),
        P("pipe", None, "dp", None),
        P("pipe", "dp", None),
        P("pipe", None),
        P("pipe", None),
    )
    return jax.shard_map(
        per_device,
        mesh=mesh,
        in_specs=placed,
        out_specs=(P("pipe", None, None), P("pipe", "dp", None)),
        check_vma=False,
    )
```

profile of v0, /device:TPU:0, one launch (start us, length us, event | category | flops | bytes accessed | tf_op | source)
XLA Modules:
  0.0 142.4 jit_solution(18307502895896163688)
XLA Ops:
  8.0 0.0 copy-start
  8.0 0.0 all-reduce.3.cloned.1.call-start
  8.1 0.8 fusion.56
  8.9 0.7 compare_and_fusion
  9.5 1.3 fusion.58
  12.2 0.1 broadcast_in_dim.27
  12.2 0.1 broadcast_in_dim.28
  12.3 1.6 %gather_fusion = bf16[4,32,2048]{2,1,0:T(8,128)(2,1)S(1)} fusion(bf16[4,32,2048]{2,1,0:T(8,128)(2,1)} %bitcast.28, s32[1024]{0:T(1024)S(1)} %pad_clamp_fusion), kind=kCustom, calls=%fused_computation | custom fusion | bytes 1048592 | tf_op jit(solution)/shard_map/jit(_take)/gather | solution.py:51
  14.0 0.1 bitcast_select_fusion
  14.1 42.3 %fusion.22 = (bf16[8192,256]{1,0:T(8,128)(2,1)S(1)}, bf16[8192,256]{1,0:T(8,128)(2,1)S(1)}) fusion(s32[]{:T(128)} %bitcast, s32[256]{0:T(256)S(1)} %get-tuple-element.144, s32[8192]{0:T(1024)S(1)} %get-tuple-element.142, s32[]{:T(128)S(6)} %mul.76, s32[256]{0:T(256)S(1)} %get-tuple-element.145, s32[8192]{0:T(1024)S(1)} %get-tuple-element.143, s32[]{:T(128)} %bitcast.1, ...), kind=kLoop, calls=%fused_computation.32 | loop fusion | flops 132120576 | bytes 8456208 | tf_op jit(solution)/shard_map/convert_element_type | solution.py:32
  56.4 0.0 copy-done
  56.4 2.4 %fusion.45 = bf16[128,512]{0,1:T(8,128)(2,1)S(1)} fusion(bf16[128,8192]{1,0:T(8,128)(2,1)S(1)} %bitcast.27, bf16[8192,256]{1,0:T(8,128)(2,1)S(1)} %get-tuple-element.139, bf16[8192,256]{1,0:T(8,128)(2,1)S(1)} %get-tuple-element.138), kind=kOutput, calls=%fused_computation.54 | convolution fusion | flops 1090584576 | bytes 10616832 | tf_op jit(solution)/shard_map/dot_general | solution.py:55
  58.8 1.3 fusion.52
  60.1 1.3 fusion.50
  61.3 0.0 all-reduce.3.cloned.1.call-update
  61.3 0.0 all-gather.2.cloned.1.call-start
  61.4 0.5 all-gather.2.cloned.1.call-update
  61.9 63.8 %all-reduce.3.cloned.1.call-done = (f32[256,1024]{1,0:T(8,128)}, f32[256,1024]{1,0:T(8,128)}) async-done(((f32[256,1024]{1,0:T(8,128)}, f32[256,1024]{1,0:T(8,128)}), (f32[256,1024]{1,0:T(8,128)}, f32[256,1024]{1,0:T(8,128)})) %all-reduce.3.cloned.1.call-update) | async-done | bytes 2097168 | tf_op jit(solution)/shard_map/psum | solution.py:60
  125.7 3.1 %maximum_bitcast_fusion = f32[1,256,2048]{2,1,0:T(8,128)} fusion(f32[256,1024]{1,0:T(8,128)} %get-tuple-element.136, f32[256,1024]{1,0:T(8,128)} %get-tuple-element.137), kind=kLoop, calls=%fused_computation.52 | loop fusion | flops 524288 | bytes 4194304 | tf_op jit(solution)/shard_map/broadcast_in_dim | solution.py:61
  128.8 0.0 copy-start.1
  128.8 0.0 all-gather.2.cloned.1.call-done
  128.8 5.2 %while.16 = (s32[]{:T(128)}, bf16[32,8192]{1,0:T(8,128)(2,1)S(1)}, s32[]{:T(128)}, bf16[4,32,8192]{2,1,0:T(8,128)(2,1)}, s32[]{:T(128)}, /*index=5*/s32[]{:T(128)}, s32[]{:T(128)}, s32[]{:T(128)}) while((s32[]{:T(128)}, bf16[32,8192]{1,0:T(8,128)(2,1)S(1)}, s32[]{:T(128)}, bf16[4,32,8192]{2,1,0:T(8,128)(2,1)}, s32[]{:T(128)}, ...), condition=%wide.region_3.4_spmd.clone, body=%wide.region_2.3_spmd.clone.sunk | while | flops 1572872 | bytes 1573019 | solution.py:22
  128.8 1.3 fusion.61
  130.2 1.3 fusion.61
  131.4 1.3 fusion.61
  132.7 1.3 fusion.61
  134.0 0.0 copy-done.1
  134.0 0.9 fusion.49
  (4 shorter events, 0.0 us)
Async XLA Ops:
  8.0 48.4 %copy-start = (bf16[1,4,32,8192]{3,2,1,0:T(8,128)(2,1)S(1)}, bf16[1,4,32,8192]{3,2,1,0:T(8,128)(2,1)}, u32[]{:S(2)}) copy-start(bf16[1,4,32,8192]{3,2,1,0:T(8,128)(2,1)} %param.7) | copy-start | bytes 6291460
  8.0 117.7 %all-reduce.3.cloned.1.call-start = ((), (), s32[]{:S(2)}) async-start(), calls=%async_computation.1 | async-start | bytes 4194304 | tf_op jit(solution)/shard_map/psum | solution.py:60
  61.3 67.5 %all-gather.2.cloned.1.call-start = ((), (), s32[]{:S(2)}) async-start(), calls=%async_computation | async-start | bytes 2621440 | tf_op jit(solution)/shard_map/all_gather | solution.py:13
  128.8 5.2 %copy-start.1 = (bf16[1,32,8192]{2,1,0:T(8,128)(2,1)S(1)}, bf16[1,32,8192]{2,1,0:T(8,128)(2,1)}, u32[]{:S(2)}) copy-start(bf16[1,32,8192]{2,1,0:T(8,128)(2,1)} %param.9) | copy-start | bytes 1572868
Sparse Core Ops, SparseCore 0:
  61.5 64.2 all-reduce.2
Sparse Core Ops, SparseCore 1:
  63.4 48.2 all-gather.1
where the time goes:
time: 143 us; the launch traced here: 142 us
  waiting for transfers between devices  64.3 us (45%)
  other arithmetic  53 us (37%)
  between operations  16.9 us (12%)
  matrix products  4.9 us (3%)
  local copies, waits for them, and re-layouts  3.11 us (2%)
    psum x1, waiting for transfers between devices, per_device(): key_total, value_total = lax.psum((key_total, value_total), 'dp')  63.8 us
    convert_element_type x1, other arithmetic, projection(): return (scaled * math.sqrt(3.0 / row_count)).astype(jnp.bfloat16)  42.3 us
    select_n x4, other arithmetic, hop(): return jnp.where(reached, new, before)  5.07 us
    broadcast_in_dim x1, other arithmetic, per_device(): compressed = jnp.concatenate([key_total, value_total], axis=1)[None]  3.09 us
  transfers between devices with their start and end apart: 2, of which 1 were waited for; matrix products, arithmetic and copies ran while one was open for 2% of the time, Pallas kernels for 0%

commit v1 on v0

v1 whole, which is shorter than its diff:
```python
import functools
import math

import jax
import jax.numpy as jnp
import ml_dtypes
import numpy as np
from jax import lax
from jax.experimental import pallas as pl
from jax.experimental.pallas import tpu as pltpu
from jax.sharding import PartitionSpec as P

PRIME = 32749
R = 256
TERMS = 32
CHUNKS = 4
DEPTH = 2


def balanced(values):
    return (values + PRIME // 2) % PRIME - PRIME // 2


def row_digits(rows):
    r = np.arange(rows, dtype=np.int64)
    a = balanced(1031 * r)
    square = balanced(a * a + 17 * r + 5)
    lines = []
    for factor in (balanced(4 * balanced(square * a)), balanced(4 * a * a + 2 * square), balanced(4 * a)):
        for place in range(3):
            rest = np.floor_divide(factor + 16, 32) if place < 2 else 0 * factor
            lines += [factor - 32 * rest] * 2
            factor = rest
    constant = balanced(square * square - PRIME // 2)
    high = np.floor_divide(constant + 128, 256)
    lines += [np.ones_like(r)] * 2 + [256 * high, constant - 256 * high]
    lines += [np.zeros_like(r)] * (TERMS - len(lines))
    return np.stack(lines).astype(ml_dtypes.bfloat16)


def reduced(values):
    quotient = jnp.round(values.astype(jnp.float32) * jnp.float32(1 / PRIME)).astype(jnp.int32)
    return values - quotient * PRIME


def column_digits(seed, columns):
    c = lax.broadcasted_iota(jnp.int32, (columns, 128), 0)
    term = lax.broadcasted_iota(jnp.int32, (columns, 128), 1)
    b = reduced(2053 * c + (3 * seed + 7))
    b2 = reduced(b * b)
    b3 = reduced(b2 * b)
    added = reduced(reduced(b2 * b2) + 29 * c + seed)
    base = jnp.where(term < 6, b, jnp.where(term < 12, b2, jnp.where(term < 18, b3, added)))
    within = jnp.where(term < 6, term, jnp.where(term < 12, term - 6, term - 12))
    place = jnp.where(term >= 18, 1, jnp.where(within < 2, 1, jnp.where(within < 4, 32, 1024)))
    whole = reduced(base * place).astype(jnp.float32)
    high = jnp.round(whole * (1 / 256)) * 256
    digit = jnp.where((term & 1) == 0, high, whole - high)
    digit = jnp.where(term >= 20, jnp.where(term < 22, 1.0, 0.0), digit)
    return digit.astype(jnp.bfloat16)


def compress_kernel(
    tile, groups, scale, halves, axis,
    seeds_hbm, plan_hbm, stash, kv_hbm, digits_hbm, keep, send,
    seeds, plan, x, kv, digits, columns, total, scalar_sem, x_sem, kv_sem, digit_sem,
):
    slots, tokens, width = stash.shape
    scalars = [
        pltpu.make_async_copy(seeds_hbm, seeds, scalar_sem.at[0]),
        pltpu.make_async_copy(plan_hbm, plan, scalar_sem.at[1]),
    ]
    for copy in scalars:
        copy.start()
    digit_copy = pltpu.make_async_copy(digits_hbm, digits, digit_sem)
    digit_copy.start()
    kv_copy = pltpu.make_async_copy(kv_hbm, kv, kv_sem)
    span = width // groups
    for copy in scalars:
        copy.wait()
    copies = [
        [
            pltpu.make_async_copy(
                stash.at[k, :, pl.ds(g * span, span)],
                x.at[plan[0, k], :, pl.ds(g * span, span)],
                x_sem.at[g, k],
            )
            for k in range(slots)
        ]
        for g in range(groups)
    ]
    for group in copies:
        for copy in group:
            copy.start()
    kv_copy.start()
    columns[0:R, :] = column_digits(seeds[0, 0], R)
    columns[R:, :] = column_digits(seeds[0, 1], R)
    digit_copy.wait()
    total[...] = jnp.zeros_like(total)
    for g in range(groups):
        for copy in copies[g]:
            copy.wait()
        for i in range(span // tile):
            part = pl.ds(g * span + i * tile, tile)
            hashed = jnp.dot(columns[:, 0:TERMS], digits[:, part], preferred_element_type=jnp.float32)
            turns = hashed * jnp.float32(1 / PRIME)
            proj = ((turns - jnp.round(turns)) * jnp.float32(scale)).astype(jnp.bfloat16)
            total[...] += lax.dot_general(
                proj, x[:, :, part].reshape(slots * tokens, tile), (((1,), (1,)), ((), ())),
                preferred_element_type=jnp.float32,
            )
    kv_copy.wait()
    half = kv.shape[2] // 2
    targets = kv[...].reshape(slots * tokens, 2 * half)
    rows = R // halves
    mine = lax.rem(lax.axis_index(axis), halves)
    for other, out in enumerate((keep, send)[:halves]):
        at = lax.rem(mine + other, halves) * rows
        for side in range(2):
            left = total[pl.ds(pl.multiple_of(side * R + at, rows), rows), :].astype(jnp.bfloat16)
            cols = slice(side * half, (side + 1) * half)
            out[:, cols] = jnp.dot(left, targets[:, cols], preferred_element_type=jnp.float32).astype(out.dtype)


def compressed_parts(stash, kv, seeds, plan, halves, axis):
    slots, tokens, width = stash.shape
    groups = 4
    tile = width // 16
    scale = PRIME * 2.0 / (PRIME - 1) * math.sqrt(3.0 / width)
    anywhere = pl.BlockSpec(memory_space=pl.ANY)
    digits = jnp.asarray(row_digits(width))
    part = (R // halves, kv.shape[2])
    return pl.pallas_call(
        functools.partial(compress_kernel, tile, groups, scale, halves, axis),
        out_shape=[jax.ShapeDtypeStruct(part, jnp.float32), jax.ShapeDtypeStruct(part, jnp.bfloat16)],
        in_specs=[anywhere] * 5,
        out_specs=[pl.BlockSpec(memory_space=pltpu.VMEM)] * 2,
        scratch_shapes=[
            pltpu.SMEM(seeds.shape, jnp.int32),
            pltpu.SMEM(plan.shape, jnp.int32),
            pltpu.VMEM((slots, tokens, width), jnp.bfloat16),
            pltpu.VMEM(kv.shape, jnp.bfloat16),
            pltpu.VMEM(digits.shape, jnp.bfloat16),
            pltpu.VMEM((2 * R, 128), jnp.bfloat16),
            pltpu.VMEM((2 * R, slots * tokens), jnp.float32),
            pltpu.SemaphoreType.DMA((2,)),
            pltpu.SemaphoreType.DMA((groups, slots)),
            pltpu.SemaphoreType.DMA,
            pltpu.SemaphoreType.DMA,
        ],
        compiler_params=pltpu.CompilerParams(vmem_limit_bytes=48 * 2**20),
        name="compress",
    )(seeds, plan, stash, kv, digits)


def exchanged(value, axis, distance):
    size = lax.axis_size(axis)
    return lax.ppermute(value, axis, [(i, i ^ distance) for i in range(size)])


def split_kernel(axis, keep, got, *outs):
    chips = len(outs)
    rows = keep.shape[0] // chips
    chip = lax.axis_index(axis) // 2
    for step, out in enumerate(outs):
        at = pl.ds(pl.multiple_of((chip ^ step) * rows, rows), rows)
        out[...] = (keep[at, :] + got[at, :].astype(jnp.float32)).astype(out.dtype)


def sum_kernel(*refs):
    *terms, out = refs
    total = terms[0][...]
    for term in terms[1:]:
        total = total + term[...].astype(jnp.float32)
    out[...] = total.astype(out.dtype)


def assemble_kernel(axis, *refs):
    *pieces, out = refs
    chips = len(pieces) // 2
    rows = pieces[0].shape[0]
    device = lax.axis_index(axis)
    for side in range(2):
        core = lax.rem(device, 2) ^ side
        for step in range(chips):
            at = (core * chips + ((device // 2) ^ step)) * rows
            out[pl.ds(pl.multiple_of(at, rows), rows), :] = pieces[side * chips + step][...].astype(out.dtype)


def vmem_call(kernel, outs, name, *args):
    inside = pl.BlockSpec(memory_space=pltpu.VMEM)
    return pl.pallas_call(
        kernel,
        out_shape=outs,
        in_specs=[inside] * len(args),
        out_specs=jax.tree.map(lambda _: inside, outs),
        compiler_params=pltpu.CompilerParams(vmem_limit_bytes=32 * 2**20),
        name=name,
    )(*args)


def summed_over(stash, kv, seeds, plan, axis):
    size = lax.axis_size(axis)
    chips = size // 2
    columns = kv.shape[2]
    small = chips in (1, 2, 4) and size == 2 * chips
    if not small:
        keep, _ = compressed_parts(stash, kv, seeds, plan, 1, axis)
        return lax.psum(keep, axis)
    keep, send = compressed_parts(stash, kv, seeds, plan, 2, axis)
    got = exchanged(send, axis, 1)
    piece = (R // size, columns)
    own, *sends = vmem_call(
        functools.partial(split_kernel, axis),
        [jax.ShapeDtypeStruct(piece, jnp.float32 if s == 0 else jnp.bfloat16) for s in range(chips)],
        "split", keep, got,
    )
    gots = [exchanged(value, axis, 2 * s) for s, value in enumerate(sends, 1)]
    done = vmem_call(sum_kernel, jax.ShapeDtypeStruct(piece, jnp.bfloat16), "sum", own, *gots)
    mine = [done] + [exchanged(done, axis, 2 * s) for s in range(1, chips)]
    theirs = [exchanged(value, axis, 1) for value in mine]
    return vmem_call(
        functools.partial(assemble_kernel, axis), jax.ShapeDtypeStruct((R, columns), jnp.float32),
        "assemble", *mine, *theirs,
    )


def added(a, b):
    return (a.astype(jnp.float32) + b.astype(jnp.float32)).astype(jnp.bfloat16)


def suffix_sums(own, axis):
    size, mine = lax.axis_size(axis), lax.axis_index(axis)
    width = own.shape[1] // CHUNKS
    chunk = [own[:, i * width:(i + 1) * width] for i in range(CHUNKS)]
    pairs = [(i, (i - 1) % size) for i in range(size)]

    def by_place(pick):
        value = pick(0)
        for place in range(1, size):
            value = jnp.where(mine == size - 1 - place, pick(place), value)
        return value

    sums, gots = [], []
    steps = CHUNKS + (size - 1) * DEPTH
    for step in range(steps):
        value = by_place(lambda place: chunk[(step - place * DEPTH) % CHUNKS])
        if step >= DEPTH:
            value = jnp.where(mine == size - 1, value, added(gots[step - DEPTH], value))
        sums.append(value)
        if step < steps - DEPTH:
            gots.append(lax.ppermute(value, axis, pairs))
    return jnp.concatenate(
        [by_place(lambda place: sums[i + place * DEPTH]) for i in range(CHUNKS)], axis=1
    )


def per_device(stashed, kv_grads, branch_grads, flora_seeds, plan):
    compressed = summed_over(stashed[0], kv_grads[0], flora_seeds, plan, "dp")
    running = suffix_sums(branch_grads[0], "pipe")
    return compressed[None], running[None]


def solution(mesh):
    placed = (
        P("pipe", None, "dp", None),
        P("pipe", None, "dp", None),
        P("pipe", "dp", None),
        P("pipe", None),
        P("pipe", None),
    )
    return jax.shard_map(
        per_device,
        mesh=mesh,
        in_specs=placed,
        out_specs=(P("pipe", None, None), P("pipe", "dp", None)),
        check_vma=False,
    )
```

time: 143 us -> 63.1 us (0.44)
  other arithmetic: 53 us -> 5.5 us
  waiting for transfers between devices: 64.3 us -> 17.1 us
  starting transfers between devices: 0.08 us -> 29.2 us
  between operations: 16.9 us -> 0.79 us
  Pallas kernels: 0 us -> 9.16 us
  matrix products: 4.9 us -> 0 us
  local copies, waits for them, and re-layouts: 3.11 us -> 1.06 us
    psum x1 -> x0, waiting for transfers between devices: 63.8 us -> none  [per_device(): key_total, value_total = lax.psum((key_total, value_total), 'dp')]
    convert_element_type x1 -> x0, other arithmetic: 42.3 us -> none  [projection(): return (scaled * math.sqrt(3.0 / row_count)).astype(jnp.bfloat16)]
    ppermute x0 -> x19, starting transfers between devices: none -> 29.2 us  [the longest x8 21.5 us: suffix_sums(): gots.append(lax.ppermute(value, axis, pairs))]
    ppermute x0 -> x19, waiting for transfers between devices: none -> 17.1 us  [the longest x11 8.82 us: exchanged(): return lax.ppermute(value, axis, [(i, i ^ distance) for i in range(size)])]
    pallas_call x0 -> x4, Pallas kernels: none -> 9.16 us  [the longest x1 7.51 us: compressed_parts(): pl.pallas_call(functools.partial(compress_kernel, tile, groups, scale, ha...]
    dot_general x3 -> x0, matrix products: 4.9 us -> none  [the longest x2 2.5 us: contract(): lax.dot_general(left_side, targets, (((0,), (0,)), ((), ())), preferred_e...]
    broadcast_in_dim x2 -> x1, other arithmetic: 4 us -> 0.83 us  [per_device(): return (compressed[None], running[None])]
    gather x1 -> x0, local copies, waits for them, and re-layouts: 1.62 us -> none  [per_device(): jnp.take(kv_grads[0], plan[0], axis=0)]
  transfers between devices with their start and end apart: 2 -> 19, of which waited for: 1 -> 9; matrix products, arithmetic and copies ran while one was open for 2% -> 2% of each run, Pallas kernels for 0% -> 12%
where the time goes in v1:
time: 63.1 us; the launch traced here: 62.8 us
  starting transfers between devices  29.2 us (46%)
  waiting for transfers between devices  17.1 us (27%)
  Pallas kernels  9.16 us (15%)
  other arithmetic  5.5 us (9%)
  local copies, waits for them, and re-layouts  1.06 us (2%)
  between operations  0.79 us (1%)
    ppermute x8, starting transfers between devices, suffix_sums(): gots.append(lax.ppermute(value, axis, pairs))  21.5 us
    ppermute x11, waiting for transfers between devices, exchanged(): return lax.ppermute(value, axis, [(i, i ^ distance) for i in range(size)])  8.82 us
    ppermute x8, waiting for transfers between devices, suffix_sums(): gots.append(lax.ppermute(value, axis, pairs))  8.25 us
    ppermute x11, starting transfers between devices, exchanged(): return lax.ppermute(value, axis, [(i, i ^ distance) for i in range(size)])  7.76 us
    pallas_call x1, Pallas kernels, compressed_parts(): pl.pallas_call(functools.partial(compress_kernel, tile, groups, scale, ha...  7.51 us
    select_n x5, other arithmetic, by_place(): value = jnp.where(mine == size - 1 - place, pick(place), value)  2.52 us
    select_n x4, other arithmetic, suffix_sums(): value = jnp.where(mine == size - 1, value, added(gots[step - DEPTH], value))  2.15 us
    pallas_call x3, Pallas kernels, vmem_call(): pl.pallas_call(kernel, out_shape=outs, in_specs=[inside] * len(args), out...  1.65 us
  transfers between devices with their start and end apart: 19, of which 9 were waited for; matrix products, arithmetic and copies ran while one was open for 2% of the time, Pallas kernels for 12%

profile of v1, /device:TPU:0, one launch (start us, length us, event | category | flops | bytes accessed | tf_op | source)
XLA Modules:
  0.0 62.8 jit_solution(5411299613233512747)
XLA Ops:
  0.7 1.1 %fusion.18 = bf16[32,2048]{1,0:T(8,128)(2,1)S(1)} fusion(pred[]{:T(512)S(6)} %eq.11, pred[]{:T(512)S(6)} %eq.10, pred[]{:T(512)S(6)} %eq.8, bf16[32,8192]{1,0:T(8,128)(2,1)} %bitcast.8), kind=kLoop, calls=%fused_computation.30 | loop fusion | flops 196608 | bytes 393219 | tf_op jit(solution)/shard_map/jit(_where)/select_n | solution.py:241
  1.8 5.1 %collective-permute-start.11 = (bf16[32,2048]{1,0:T(8,128)(2,1)S(1)}, bf16[32,2048]{1,0:T(8,128)(2,1)S(1)}, u32[]{:S(2)}, u32[]{:S(2)}) collective-permute-start(bf16[32,2048]{1,0:T(8,128)(2,1)S(1)} %fusion.18), channel_id=1, source_target_pairs={{0,3},{1,0},{2,1},{3,2},{4,7},{5,4},{6,5},{7,6},{8,11},{9,8},{10,9... | collective-permute-start | bytes 393224 | tf_op jit(solution)/shard_map/ppermute | solution.py:252
  6.9 2.8 %collective-permute-done.11 = bf16[32,2048]{1,0:T(8,128)(2,1)S(1)} collective-permute-done((bf16[32,2048]{1,0:T(8,128)(2,1)S(1)}, bf16[32,2048]{1,0:T(8,128)(2,1)S(1)}, u32[]{:S(2)}, u32[]{:S(2)}) %collective-permute-start.11) | collective-permute-done | bytes 131104 | tf_op jit(solution)/shard_map/ppermute | solution.py:252
  9.7 1.0 %fusion.15 = bf16[32,2048]{1,0:T(8,128)(2,1)S(1)} fusion(bf16[32,2048]{1,0:T(8,128)(2,1)S(1)} %collective-permute-done.11, pred[]{:T(512)S(6)} %eq.9, pred[]{:T(512)S(6)} %eq.11, bf16[32,8192]{1,0:T(8,128)(2,1)} %bitcast.9, pred[]{:T(512)S(6)} %eq.10, pred[]{:T(512)S(6)} %eq.8), kind=kLoop, calls=%fused_computation.24 | loop fusion | flops 524288 | bytes 524292 | tf_op jit(solution)/shard_map/jit(_where)/select_n | solution.py:249
  10.7 4.3 %collective-permute-start.12 = (bf16[32,2048]{1,0:T(8,128)(2,1)S(1)}, bf16[32,2048]{1,0:T(8,128)(2,1)S(1)}, u32[]{:S(2)}, u32[]{:S(2)}) collective-permute-start(bf16[32,2048]{1,0:T(8,128)(2,1)S(1)} %fusion.15), channel_id=1, source_target_pairs={{0,3},{1,0},{2,1},{3,2},{4,7},{5,4},{6,5},{7,6},{8,11},{9,8},{10,9... | collective-permute-start | bytes 393224 | tf_op jit(solution)/shard_map/ppermute | solution.py:252
  15.0 2.5 %collective-permute-done.12 = bf16[32,2048]{1,0:T(8,128)(2,1)S(1)} collective-permute-done((bf16[32,2048]{1,0:T(8,128)(2,1)S(1)}, bf16[32,2048]{1,0:T(8,128)(2,1)S(1)}, u32[]{:S(2)}, u32[]{:S(2)}) %collective-permute-start.12) | collective-permute-done | bytes 131104 | tf_op jit(solution)/shard_map/ppermute | solution.py:252
  17.6 1.0 %fusion.13 = bf16[32,2048]{1,0:T(8,128)(2,1)S(1)} fusion(bf16[32,2048]{1,0:T(8,128)(2,1)S(1)} %collective-permute-done.12, pred[]{:T(512)S(6)} %eq.9, pred[]{:T(512)S(6)} %eq.11, bf16[32,8192]{1,0:T(8,128)(2,1)} %bitcast.10, pred[]{:T(512)S(6)} %eq.10, pred[]{:T(512)S(6)} %eq.8), kind=kLoop, calls=%fused_computation.22 | loop fusion | flops 524288 | bytes 524292 | tf_op jit(solution)/shard_map/jit(_where)/select_n | solution.py:249
  18.6 4.3 %collective-permute-start.13 = (bf16[32,2048]{1,0:T(8,128)(2,1)S(1)}, bf16[32,2048]{1,0:T(8,128)(2,1)S(1)}, u32[]{:S(2)}, u32[]{:S(2)}) collective-permute-start(bf16[32,2048]{1,0:T(8,128)(2,1)S(1)} %fusion.13), channel_id=1, source_target_pairs={{0,3},{1,0},{2,1},{3,2},{4,7},{5,4},{6,5},{7,6},{8,11},{9,8},{10,9... | collective-permute-start | bytes 393224 | tf_op jit(solution)/shard_map/ppermute | solution.py:252
  22.9 2.5 %collective-permute-done.13 = bf16[32,2048]{1,0:T(8,128)(2,1)S(1)} collective-permute-done((bf16[32,2048]{1,0:T(8,128)(2,1)S(1)}, bf16[32,2048]{1,0:T(8,128)(2,1)S(1)}, u32[]{:S(2)}, u32[]{:S(2)}) %collective-permute-start.13) | collective-permute-done | bytes 131104 | tf_op jit(solution)/shard_map/ppermute | solution.py:252
  25.4 1.2 %select_select_fusion.5 = (bf16[32,2048]{1,0:T(8,128)(2,1)S(1)}, bf16[32,2048]{1,0:T(8,128)(2,1)S(1)}, bf16[32,2048]{1,0:T(8,128)(2,1)S(1)}) fusion(bf16[32,2048]{1,0:T(8,128)(2,1)S(1)} %fusion.13, bf16[32,2048]{1,0:T(8,128)(2,1)S(1)} %fusion.15, pred[]{:T(512)S(6)} %eq.11, pred[]{:T(512)S(6)} %eq.10, pred[]{:T(512)S(6)} %eq.8, ...), kind=kLoop, calls=%fused_computation.36 | loop fusion | flops 1114112 | bytes 1310724 | tf_op jit(solution)/shard_map/jit(_where)/select_n | solution.py:241
  26.6 4.3 %collective-permute-start.14 = (bf16[32,2048]{1,0:T(8,128)(2,1)S(1)}, bf16[32,2048]{1,0:T(8,128)(2,1)S(1)}, u32[]{:S(2)}, u32[]{:S(2)}) collective-permute-start(bf16[32,2048]{1,0:T(8,128)(2,1)S(1)} %get-tuple-element.18), channel_id=1, source_target_pairs={{0,3},{1,0},{2,1},{3,2},{4,7},{5,4},{6,5},{7,6},{8,11},{9,8},{10,9... | collective-permute-start | bytes 393224 | tf_op jit(solution)/shard_map/ppermute | solution.py:252
  30.9 1.0 %copy-done.2 = bf16[32,8192]{1,0:T(8,128)(2,1)S(1)} copy-done((bf16[32,8192]{1,0:T(8,128)(2,1)S(1)}, bf16[32,8192]{1,0:T(8,128)(2,1)}, u32[]{:S(2)}) %copy-start.2) | copy-done | bytes 524312
  32.0 7.5 %compress.1 = (f32[128,2048]{1,0:T(8,128)S(1)}, bf16[128,2048]{1,0:T(8,128)(2,1)S(1)}) custom-call(s32[1,2]{1,0:T(1,128)S(1)} %copy-done.3, s32[1,4]{1,0:T(1,128)S(1)} %copy-done.4, bf16[4,32,8192]{2,1,0:T(8,128)(2,1)S(1)} %bitcast.6, bf16[4,32,2048]{2,1,0:T(8,128)(2,1)S(1)} %bitcast.7, bf16[32,8192]{1,0:T(8,128)(2,1)S(1)} %copy-done.2), custom_call_target="tpu_custom_call" | custom-call | tf_op jit(solution)/shard_map/compress/pallas_call | solution.py:133
  39.6 0.1 collective-permute-start.15
  39.7 1.7 %collective-permute-done.got = bf16[128,2048]{1,0:T(8,128)(2,1)S(1)} collective-permute-done((bf16[128,2048]{1,0:T(8,128)(2,1)S(1)}, bf16[128,2048]{1,0:T(8,128)(2,1)S(1)}, u32[]{:S(2)}, u32[]{:S(2)}) %collective-permute-start) | collective-permute-done | bytes 524320 | tf_op jit(solution)/shard_map/ppermute | solution.py:158
  41.5 0.1 split.1
  41.6 1.6 %collective-permute-start.1 = (bf16[32,2048]{1,0:T(8,128)(2,1)S(1)}, bf16[32,2048]{1,0:T(8,128)(2,1)S(1)}, u32[]{:S(2)}, u32[]{:S(2)}) collective-permute-start(bf16[32,2048]{1,0:T(8,128)(2,1)S(1)} %get-tuple-element.11), channel_id=1, source_target_pairs={{0,8},{4,12},{8,0},{12,4},{16,24},{20,28},{24,16},{28,20},{1,9},{5... | collective-permute-start | bytes 393224 | tf_op jit(solution)/shard_map/ppermute | solution.py:158
  43.1 1.5 %collective-permute-start.2 = (bf16[32,2048]{1,0:T(8,128)(2,1)S(1)}, bf16[32,2048]{1,0:T(8,128)(2,1)S(1)}, u32[]{:S(2)}, u32[]{:S(2)}) collective-permute-start(bf16[32,2048]{1,0:T(8,128)(2,1)S(1)} %get-tuple-element.12), channel_id=1, source_target_pairs={{0,16},{4,20},{8,24},{12,28},{16,0},{20,4},{24,8},{28,12},{1,17},{... | collective-permute-start | bytes 393224 | tf_op jit(solution)/shard_map/ppermute | solution.py:158
  44.7 0.5 collective-permute-start.3
  45.1 0.4 collective-permute-done.15
  45.6 2.1 %collective-permute-start.16 = (bf16[32,2048]{1,0:T(8,128)(2,1)S(1)}, bf16[32,2048]{1,0:T(8,128)(2,1)S(1)}, u32[]{:S(2)}, u32[]{:S(2)}) collective-permute-start(bf16[32,2048]{1,0:T(8,128)(2,1)S(1)} %fusion.9), channel_id=1, source_target_pairs={{0,3},{1,0},{2,1},{3,2},{4,7},{5,4},{6,5},{7,6},{8,11},{9,8},{10,9... | collective-permute-start | bytes 393224 | tf_op jit(solution)/shard_map/ppermute | solution.py:252
  47.8 3.4 %collective-permute-done.2.refs_2_ = bf16[32,2048]{1,0:T(8,128)(2,1)S(1)} collective-permute-done((bf16[32,2048]{1,0:T(8,128)(2,1)S(1)}, bf16[32,2048]{1,0:T(8,128)(2,1)S(1)}, u32[]{:S(2)}, u32[]{:S(2)}) %collective-permute-start.2) | collective-permute-done | bytes 131104 | tf_op jit(solution)/shard_map/ppermute | solution.py:158
  51.3 1.3 %collective-permute-start.4 = (bf16[32,2048]{1,0:T(8,128)(2,1)S(1)}, bf16[32,2048]{1,0:T(8,128)(2,1)S(1)}, u32[]{:S(2)}, u32[]{:S(2)}) collective-permute-start(bf16[32,2048]{1,0:T(8,128)(2,1)S(1)} %sum.1.refs_0_), channel_id=1, source_target_pairs={{0,8},{4,12},{8,0},{12,4},{16,24},{20,28},{24,16},{28,20},{1,9},{5... | collective-permute-start | bytes 393224 | tf_op jit(solution)/shard_map/ppermute | solution.py:158
  52.6 0.8 %collective-permute-start.5 = (bf16[32,2048]{1,0:T(8,128)(2,1)S(1)}, bf16[32,2048]{1,0:T(8,128)(2,1)S(1)}, u32[]{:S(2)}, u32[]{:S(2)}) collective-permute-start(bf16[32,2048]{1,0:T(8,128)(2,1)S(1)} %sum.1.refs_0_), channel_id=1, source_target_pairs={{0,16},{4,20},{8,24},{12,28},{16,0},{20,4},{24,8},{28,12},{1,17},{... | collective-permute-start | bytes 393224 | tf_op jit(solution)/shard_map/ppermute | solution.py:158
  53.4 1.4 %collective-permute-start.6 = (bf16[32,2048]{1,0:T(8,128)(2,1)S(1)}, bf16[32,2048]{1,0:T(8,128)(2,1)S(1)}, u32[]{:S(2)}, u32[]{:S(2)}) collective-permute-start(bf16[32,2048]{1,0:T(8,128)(2,1)S(1)} %sum.1.refs_0_), channel_id=1, source_target_pairs={{0,24},{4,28},{8,16},{12,20},{16,8},{20,12},{24,0},{28,4},{1,25},{... | collective-permute-start | bytes 393224 | tf_op jit(solution)/shard_map/ppermute | solution.py:158
  54.9 1.2 %collective-permute-start.18 = (bf16[32,2048]{1,0:T(8,128)(2,1)S(1)}, bf16[32,2048]{1,0:T(8,128)(2,1)S(1)}, u32[]{:S(2)}, u32[]{:S(2)}) collective-permute-start(bf16[32,2048]{1,0:T(8,128)(2,1)S(1)} %get-tuple-element.17), channel_id=1, source_target_pairs={{0,3},{1,0},{2,1},{3,2},{4,7},{5,4},{6,5},{7,6},{8,11},{9,8},{10,9... | collective-permute-start | bytes 393224 | tf_op jit(solution)/shard_map/ppermute | solution.py:252
  56.2 1.1 %collective-permute-done.4.refs_1_ = bf16[32,2048]{1,0:T(8,128)(2,1)S(1)} collective-permute-done((bf16[32,2048]{1,0:T(8,128)(2,1)S(1)}, bf16[32,2048]{1,0:T(8,128)(2,1)S(1)}, u32[]{:S(2)}, u32[]{:S(2)}) %collective-permute-start.4) | collective-permute-done | bytes 131104 | tf_op jit(solution)/shard_map/ppermute | solution.py:158
  57.3 2.5 %collective-permute-done.5.refs_2_ = bf16[32,2048]{1,0:T(8,128)(2,1)S(1)} collective-permute-done((bf16[32,2048]{1,0:T(8,128)(2,1)S(1)}, bf16[32,2048]{1,0:T(8,128)(2,1)S(1)}, u32[]{:S(2)}, u32[]{:S(2)}) %collective-permute-start.5) | collective-permute-done | bytes 131104 | tf_op jit(solution)/shard_map/ppermute | solution.py:158
  59.8 0.5 collective-permute-start.10
  60.4 0.8 %maximum_bitcast_fusion = bf16[1,32,8192]{2,1,0:T(8,128)(2,1)} fusion(bf16[32,2048]{1,0:T(8,128)(2,1)S(1)} %fusion.21, bf16[32,2048]{1,0:T(8,128)(2,1)S(1)} %fusion.20, bf16[32,2048]{1,0:T(8,128)(2,1)S(1)} %get-tuple-element.16, bf16[32,2048]{1,0:T(8,128)(2,1)S(1)} %get-tuple-element.14), kind=kLoop, calls=%fused_computation | loop fusion | flops 2097152 | bytes 1048576 | tf_op jit(solution)/shard_map/broadcast_in_dim | solution.py:261
  61.2 0.1 collective-permute-done.10.refs_7_
  61.3 1.5 %assemble.1 = f32[256,2048]{1,0:T(8,128)} custom-call(bf16[32,2048]{1,0:T(8,128)(2,1)S(1)} %sum.1.refs_0_, bf16[32,2048]{1,0:T(8,128)(2,1)S(1)} %collective-permute-done.4.refs_1_, bf16[32,2048]{1,0:T(8,128)(2,1)S(1)} %collective-permute-done.5.refs_2_, bf16[32,2048]{1,0:T(8,128)(2,1)S(1)} %collective-permute-done.6.refs_3_, ...), custom_call_target="tpu_custom_call" | custom-call | tf_op jit(solution)/shard_map/assemble/pallas_call | solution.py:192
  (32 shorter events, 0.6 us)
Async XLA Ops:
  0.6 30.3 %copy-start.3 = (s32[1,2]{1,0:T(1,128)S(1)}, s32[1,2]{1,0:T(1,128)}, u32[]{:S(2)}) copy-start(s32[1,2]{1,0:T(1,128)} %seeds_hbm.1) | copy-start | bytes 28
  0.6 30.3 %copy-start.4 = (s32[1,4]{1,0:T(1,128)S(1)}, s32[1,4]{1,0:T(1,128)}, u32[]{:S(2)}) copy-start(s32[1,4]{1,0:T(1,128)} %plan_hbm.1) | copy-start | bytes 52
  0.7 30.3 %copy-start = (bf16[1,4,32,8192]{3,2,1,0:T(8,128)(2,1)S(1)}, bf16[1,4,32,8192]{3,2,1,0:T(8,128)(2,1)}, u32[]{:S(2)}) copy-start(bf16[1,4,32,8192]{3,2,1,0:T(8,128)(2,1)} %param.6) | copy-start | bytes 6291460
  0.7 30.2 %copy-start.1 = (bf16[1,4,32,2048]{3,2,1,0:T(8,128)(2,1)S(1)}, bf16[1,4,32,2048]{3,2,1,0:T(8,128)(2,1)}, u32[]{:S(2)}) copy-start(bf16[1,4,32,2048]{3,2,1,0:T(8,128)(2,1)} %param.7) | copy-start | bytes 1572868
  1.8 7.9 %collective-permute-start.11 = (bf16[32,2048]{1,0:T(8,128)(2,1)S(1)}, bf16[32,2048]{1,0:T(8,128)(2,1)S(1)}, u32[]{:S(2)}, u32[]{:S(2)}) collective-permute-start(bf16[32,2048]{1,0:T(8,128)(2,1)S(1)} %fusion.18), channel_id=1, source_target_pairs={{0,3},{1,0},{2,1},{3,2},{4,7},{5,4},{6,5},{7,6},{8,11},{9,8},{10,9... | collective-permute-start | bytes 393224 | tf_op jit(solution)/shard_map/ppermute | solution.py:252
  10.7 6.9 %collective-permute-start.12 = (bf16[32,2048]{1,0:T(8,128)(2,1)S(1)}, bf16[32,2048]{1,0:T(8,128)(2,1)S(1)}, u32[]{:S(2)}, u32[]{:S(2)}) collective-permute-start(bf16[32,2048]{1,0:T(8,128)(2,1)S(1)} %fusion.15), channel_id=1, source_target_pairs={{0,3},{1,0},{2,1},{3,2},{4,7},{5,4},{6,5},{7,6},{8,11},{9,8},{10,9... | collective-permute-start | bytes 393224 | tf_op jit(solution)/shard_map/ppermute | solution.py:252
  18.6 6.8 %collective-permute-start.13 = (bf16[32,2048]{1,0:T(8,128)(2,1)S(1)}, bf16[32,2048]{1,0:T(8,128)(2,1)S(1)}, u32[]{:S(2)}, u32[]{:S(2)}) collective-permute-start(bf16[32,2048]{1,0:T(8,128)(2,1)S(1)} %fusion.13), channel_id=1, source_target_pairs={{0,3},{1,0},{2,1},{3,2},{4,7},{5,4},{6,5},{7,6},{8,11},{9,8},{10,9... | collective-permute-start | bytes 393224 | tf_op jit(solution)/shard_map/ppermute | solution.py:252
  26.6 13.0 %collective-permute-start.14 = (bf16[32,2048]{1,0:T(8,128)(2,1)S(1)}, bf16[32,2048]{1,0:T(8,128)(2,1)S(1)}, u32[]{:S(2)}, u32[]{:S(2)}) collective-permute-start(bf16[32,2048]{1,0:T(8,128)(2,1)S(1)} %get-tuple-element.18), channel_id=1, source_target_pairs={{0,3},{1,0},{2,1},{3,2},{4,7},{5,4},{6,5},{7,6},{8,11},{9,8},{10,9... | collective-permute-start | bytes 393224 | tf_op jit(solution)/shard_map/ppermute | solution.py:252
  30.9 1.0 %copy-start.2 = (bf16[32,8192]{1,0:T(8,128)(2,1)S(1)}, bf16[32,8192]{1,0:T(8,128)(2,1)}, u32[]{:S(2)}) copy-start(bf16[32,8192]{1,0:T(8,128)(2,1)} %constant.14.clone.digits_hbm) | copy-start | bytes 1572868
  32.0 7.6 %copy-start.5 = (bf16[1,32,8192]{2,1,0:T(8,128)(2,1)S(1)}, bf16[1,32,8192]{2,1,0:T(8,128)(2,1)}, u32[]{:S(2)}) copy-start(bf16[1,32,8192]{2,1,0:T(8,128)(2,1)} %param.8) | copy-start | bytes 1572868
  39.5 2.0 %collective-permute-start = (bf16[128,2048]{1,0:T(8,128)(2,1)S(1)}, bf16[128,2048]{1,0:T(8,128)(2,1)S(1)}, u32[]{:S(2)}, u32[]{:S(2)}) collective-permute-start(bf16[128,2048]{1,0:T(8,128)(2,1)S(1)} %get-tuple-element.9), channel_id=1, source_target_pairs={{0,4},{4,0},{8,12},{12,8},{16,20},{20,16},{24,28},{28,24},{1,5},{5... | collective-permute-start | bytes 1572872 | tf_op jit(solution)/shard_map/ppermute | solution.py:158
  39.6 5.9 %collective-permute-start.15 = (bf16[32,2048]{1,0:T(8,128)(2,1)S(1)}, bf16[32,2048]{1,0:T(8,128)(2,1)S(1)}, u32[]{:S(2)}, u32[]{:S(2)}) collective-permute-start(bf16[32,2048]{1,0:T(8,128)(2,1)S(1)} %fusion.11), channel_id=1, source_target_pairs={{0,3},{1,0},{2,1},{3,2},{4,7},{5,4},{6,5},{7,6},{8,11},{9,8},{10,9... | collective-permute-start | bytes 393224 | tf_op jit(solution)/shard_map/ppermute | solution.py:252
  41.6 6.2 %collective-permute-start.1 = (bf16[32,2048]{1,0:T(8,128)(2,1)S(1)}, bf16[32,2048]{1,0:T(8,128)(2,1)S(1)}, u32[]{:S(2)}, u32[]{:S(2)}) collective-permute-start(bf16[32,2048]{1,0:T(8,128)(2,1)S(1)} %get-tuple-element.11), channel_id=1, source_target_pairs={{0,8},{4,12},{8,0},{12,4},{16,24},{20,28},{24,16},{28,20},{1,9},{5... | collective-permute-start | bytes 393224 | tf_op jit(solution)/shard_map/ppermute | solution.py:158
  43.1 8.1 %collective-permute-start.2 = (bf16[32,2048]{1,0:T(8,128)(2,1)S(1)}, bf16[32,2048]{1,0:T(8,128)(2,1)S(1)}, u32[]{:S(2)}, u32[]{:S(2)}) collective-permute-start(bf16[32,2048]{1,0:T(8,128)(2,1)S(1)} %get-tuple-element.12), channel_id=1, source_target_pairs={{0,16},{4,20},{8,24},{12,28},{16,0},{20,4},{24,8},{28,12},{1,17},{... | collective-permute-start | bytes 393224 | tf_op jit(solution)/shard_map/ppermute | solution.py:158
  44.7 6.6 %collective-permute-start.3 = (bf16[32,2048]{1,0:T(8,128)(2,1)S(1)}, bf16[32,2048]{1,0:T(8,128)(2,1)S(1)}, u32[]{:S(2)}, u32[]{:S(2)}) collective-permute-start(bf16[32,2048]{1,0:T(8,128)(2,1)S(1)} %get-tuple-element.13), channel_id=1, source_target_pairs={{0,24},{4,28},{8,16},{12,20},{16,8},{20,12},{24,0},{28,4},{1,25},{... | collective-permute-start | bytes 393224 | tf_op jit(solution)/shard_map/ppermute | solution.py:158
  45.6 9.2 %collective-permute-start.16 = (bf16[32,2048]{1,0:T(8,128)(2,1)S(1)}, bf16[32,2048]{1,0:T(8,128)(2,1)S(1)}, u32[]{:S(2)}, u32[]{:S(2)}) collective-permute-start(bf16[32,2048]{1,0:T(8,128)(2,1)S(1)} %fusion.9), channel_id=1, source_target_pairs={{0,3},{1,0},{2,1},{3,2},{4,7},{5,4},{6,5},{7,6},{8,11},{9,8},{10,9... | collective-permute-start | bytes 393224 | tf_op jit(solution)/shard_map/ppermute | solution.py:252
  47.8 8.3 %collective-permute-start.17 = (bf16[32,2048]{1,0:T(8,128)(2,1)S(1)}, bf16[32,2048]{1,0:T(8,128)(2,1)S(1)}, u32[]{:S(2)}, u32[]{:S(2)}) collective-permute-start(bf16[32,2048]{1,0:T(8,128)(2,1)S(1)} %get-tuple-element.15), channel_id=1, source_target_pairs={{0,3},{1,0},{2,1},{3,2},{4,7},{5,4},{6,5},{7,6},{8,11},{9,8},{10,9... | collective-permute-start | bytes 393224 | tf_op jit(solution)/shard_map/ppermute | solution.py:252
  51.3 6.0 %collective-permute-start.4 = (bf16[32,2048]{1,0:T(8,128)(2,1)S(1)}, bf16[32,2048]{1,0:T(8,128)(2,1)S(1)}, u32[]{:S(2)}, u32[]{:S(2)}) collective-permute-start(bf16[32,2048]{1,0:T(8,128)(2,1)S(1)} %sum.1.refs_0_), channel_id=1, source_target_pairs={{0,8},{4,12},{8,0},{12,4},{16,24},{20,28},{24,16},{28,20},{1,9},{5... | collective-permute-start | bytes 393224 | tf_op jit(solution)/shard_map/ppermute | solution.py:158
  52.6 7.2 %collective-permute-start.5 = (bf16[32,2048]{1,0:T(8,128)(2,1)S(1)}, bf16[32,2048]{1,0:T(8,128)(2,1)S(1)}, u32[]{:S(2)}, u32[]{:S(2)}) collective-permute-start(bf16[32,2048]{1,0:T(8,128)(2,1)S(1)} %sum.1.refs_0_), channel_id=1, source_target_pairs={{0,16},{4,20},{8,24},{12,28},{16,0},{20,4},{24,8},{28,12},{1,17},{... | collective-permute-start | bytes 393224 | tf_op jit(solution)/shard_map/ppermute | solution.py:158
  53.4 6.4 %collective-permute-start.6 = (bf16[32,2048]{1,0:T(8,128)(2,1)S(1)}, bf16[32,2048]{1,0:T(8,128)(2,1)S(1)}, u32[]{:S(2)}, u32[]{:S(2)}) collective-permute-start(bf16[32,2048]{1,0:T(8,128)(2,1)S(1)} %sum.1.refs_0_), channel_id=1, source_target_pairs={{0,24},{4,28},{8,16},{12,20},{16,8},{20,12},{24,0},{28,4},{1,25},{... | collective-permute-start | bytes 393224 | tf_op jit(solution)/shard_map/ppermute | solution.py:158
  54.9 5.4 %collective-permute-start.18 = (bf16[32,2048]{1,0:T(8,128)(2,1)S(1)}, bf16[32,2048]{1,0:T(8,128)(2,1)S(1)}, u32[]{:S(2)}, u32[]{:S(2)}) collective-permute-start(bf16[32,2048]{1,0:T(8,128)(2,1)S(1)} %get-tuple-element.17), channel_id=1, source_target_pairs={{0,3},{1,0},{2,1},{3,2},{4,7},{5,4},{6,5},{7,6},{8,11},{9,8},{10,9... | collective-permute-start | bytes 393224 | tf_op jit(solution)/shard_map/ppermute | solution.py:252
  56.1 5.1 %collective-permute-start.7 = (bf16[32,2048]{1,0:T(8,128)(2,1)S(1)}, bf16[32,2048]{1,0:T(8,128)(2,1)S(1)}, u32[]{:S(2)}, u32[]{:S(2)}) collective-permute-start(bf16[32,2048]{1,0:T(8,128)(2,1)S(1)} %sum.1.refs_0_), channel_id=1, source_target_pairs={{0,4},{4,0},{8,12},{12,8},{16,20},{20,16},{24,28},{28,24},{1,5},{5... | collective-permute-start | bytes 393224 | tf_op jit(solution)/shard_map/ppermute | solution.py:158
  57.3 3.9 %collective-permute-start.8 = (bf16[32,2048]{1,0:T(8,128)(2,1)S(1)}, bf16[32,2048]{1,0:T(8,128)(2,1)S(1)}, u32[]{:S(2)}, u32[]{:S(2)}) collective-permute-start(bf16[32,2048]{1,0:T(8,128)(2,1)S(1)} %collective-permute-done.4.refs_1_), channel_id=1, source_target_pairs={{0,4},{4,0},{8,12},{12,8},{16,20},{20,16},{24,28},{28,24},{1,5},{5... | collective-permute-start | bytes 393224 | tf_op jit(solution)/shard_map/ppermute | solution.py:158
  59.8 1.4 %collective-permute-start.9 = (bf16[32,2048]{1,0:T(8,128)(2,1)S(1)}, bf16[32,2048]{1,0:T(8,128)(2,1)S(1)}, u32[]{:S(2)}, u32[]{:S(2)}) collective-permute-start(bf16[32,2048]{1,0:T(8,128)(2,1)S(1)} %collective-permute-done.5.refs_2_), channel_id=1, source_target_pairs={{0,4},{4,0},{8,12},{12,8},{16,20},{20,16},{24,28},{28,24},{1,5},{5... | collective-permute-start | bytes 393224 | tf_op jit(solution)/shard_map/ppermute | solution.py:158
  59.8 1.5 %collective-permute-start.10 = (bf16[32,2048]{1,0:T(8,128)(2,1)S(1)}, bf16[32,2048]{1,0:T(8,128)(2,1)S(1)}, u32[]{:S(2)}, u32[]{:S(2)}) collective-permute-start(bf16[32,2048]{1,0:T(8,128)(2,1)S(1)} %collective-permute-done.6.refs_3_), channel_id=1, source_target_pairs={{0,4},{4,0},{8,12},{12,8},{16,20},{20,16},{24,28},{28,24},{1,5},{5... | collective-permute-start | bytes 393224 | tf_op jit(solution)/shard_map/ppermute | solution.py:158

commit v2 on v1

v2 whole, which is shorter than its diff:
```python
import functools
import math

import jax
import jax.numpy as jnp
import ml_dtypes
import numpy as np
from jax import lax
from jax.experimental import pallas as pl
from jax.experimental.pallas import tpu as pltpu
from jax.sharding import PartitionSpec as P

PRIME = 32749
R = 256
TERMS = 32


def balanced(values):
    return (values + PRIME // 2) % PRIME - PRIME // 2


def row_digits(rows):
    r = np.arange(rows, dtype=np.int64)
    a = balanced(1031 * r)
    square = balanced(a * a + 17 * r + 5)
    lines = []
    for factor in (balanced(4 * balanced(square * a)), balanced(4 * a * a + 2 * square), balanced(4 * a)):
        for place in range(3):
            rest = np.floor_divide(factor + 16, 32) if place < 2 else 0 * factor
            lines += [factor - 32 * rest] * 2
            factor = rest
    constant = balanced(square * square - PRIME // 2)
    high = np.floor_divide(constant + 128, 256)
    lines += [np.ones_like(r)] * 2 + [256 * high, constant - 256 * high]
    lines += [np.zeros_like(r)] * (TERMS - len(lines))
    return np.stack(lines).astype(ml_dtypes.bfloat16)


def reduced(values):
    quotient = jnp.round(values.astype(jnp.float32) * jnp.float32(1 / PRIME)).astype(jnp.int32)
    return values - quotient * PRIME


def column_digits(seed, columns):
    c = lax.broadcasted_iota(jnp.int32, (columns, 128), 0)
    term = lax.broadcasted_iota(jnp.int32, (columns, 128), 1)
    b = reduced(2053 * c + (3 * seed + 7))
    b2 = reduced(b * b)
    b3 = reduced(b2 * b)
    added = reduced(reduced(b2 * b2) + 29 * c + seed)
    base = jnp.where(term < 6, b, jnp.where(term < 12, b2, jnp.where(term < 18, b3, added)))
    within = jnp.where(term < 6, term, jnp.where(term < 12, term - 6, term - 12))
    place = jnp.where(term >= 18, 1, jnp.where(within < 2, 1, jnp.where(within < 4, 32, 1024)))
    whole = reduced(base * place).astype(jnp.float32)
    high = jnp.round(whole * (1 / 256)) * 256
    digit = jnp.where((term & 1) == 0, high, whole - high)
    digit = jnp.where(term >= 20, jnp.where(term < 22, 1.0, 0.0), digit)
    return digit.astype(jnp.bfloat16)


def compress_kernel(
    tile, groups, scale, halves, axis,
    seeds_hbm, plan_hbm, stash, kv_hbm, digits_hbm, kept, send,
    seeds, plan, x, kv, digits, columns, total, scalar_sem, x_sem, kv_sem, digit_sem,
):
    slots, tokens, width = stash.shape
    span = width // groups
    scalars = [
        pltpu.make_async_copy(seeds_hbm, seeds, scalar_sem.at[0]),
        pltpu.make_async_copy(plan_hbm, plan, scalar_sem.at[1]),
    ]
    digit_copy = pltpu.make_async_copy(digits_hbm, digits, digit_sem)
    copies = [
        pltpu.make_async_copy(
            stash.at[:, :, pl.ds(g * span, span)], x.at[:, :, pl.ds(g * span, span)], x_sem.at[g]
        )
        for g in range(groups)
    ]
    for copy in (*scalars, digit_copy, *copies):
        copy.start()
    for copy in scalars:
        copy.wait()
    kv_copies = [
        pltpu.make_async_copy(kv_hbm.at[plan[0, k]], kv.at[k], kv_sem.at[k]) for k in range(slots)
    ]
    for copy in kv_copies:
        copy.start()
    columns[0:R, :] = column_digits(seeds[0, 0], R)
    columns[R:, :] = column_digits(seeds[0, 1], R)
    digit_copy.wait()
    total[...] = jnp.zeros_like(total)
    for g in range(groups):
        copies[g].wait()
        for i in range(span // tile):
            part = pl.ds(g * span + i * tile, tile)
            hashed = jnp.dot(columns[:, 0:TERMS], digits[:, part], preferred_element_type=jnp.float32)
            turns = hashed * jnp.float32(1 / PRIME)
            proj = ((turns - jnp.round(turns)) * jnp.float32(scale)).astype(jnp.bfloat16)
            total[...] += lax.dot_general(
                proj, x[:, :, part].reshape(slots * tokens, tile), (((1,), (1,)), ((), ())),
                preferred_element_type=jnp.float32,
            )
    for copy in kv_copies:
        copy.wait()
    half = kv.shape[2] // 2
    targets = kv[...].reshape(slots * tokens, 2 * half)
    rows = R // halves
    mine = lax.rem(lax.axis_index(axis), halves)
    for side in range(2):
        kept[side] = total[pl.ds(pl.multiple_of(side * R + mine * rows, rows), rows), :].astype(jnp.bfloat16)
        if halves > 1:
            other = pl.multiple_of(side * R + (1 - mine) * rows, rows)
            left = total[pl.ds(other, rows), :].astype(jnp.bfloat16)
            cols = slice(side * half, (side + 1) * half)
            send[:, cols] = jnp.dot(
                left, targets[:, cols], preferred_element_type=jnp.float32
            ).astype(send.dtype)


def keep_kernel(plan_hbm, kv_hbm, kept, out, plan, kv, plan_sem, kv_sem):
    slots, tokens, width = kv.shape
    plan_copy = pltpu.make_async_copy(plan_hbm, plan, plan_sem)
    plan_copy.start()
    plan_copy.wait()
    copies = [pltpu.make_async_copy(kv_hbm.at[plan[0, k]], kv.at[k], kv_sem.at[k]) for k in range(slots)]
    for copy in copies:
        copy.start()
    for copy in copies:
        copy.wait()
    targets = kv[...].reshape(slots * tokens, width)
    for side in range(2):
        cols = slice(side * width // 2, (side + 1) * width // 2)
        out[:, cols] = jnp.dot(kept[side], targets[:, cols], preferred_element_type=jnp.float32)


def kept_part(plan, kv, kept):
    inside, far = pl.BlockSpec(memory_space=pltpu.VMEM), pl.BlockSpec(memory_space=pl.ANY)
    return pl.pallas_call(
        keep_kernel,
        out_shape=jax.ShapeDtypeStruct((kept.shape[1], kv.shape[2]), jnp.float32),
        in_specs=[far, far, inside],
        out_specs=inside,
        scratch_shapes=[
            pltpu.SMEM(plan.shape, jnp.int32),
            pltpu.VMEM(kv.shape, jnp.bfloat16),
            pltpu.SemaphoreType.DMA,
            pltpu.SemaphoreType.DMA((kv.shape[0],)),
        ],
        compiler_params=pltpu.CompilerParams(vmem_limit_bytes=16 * 2**20),
        cost_estimate=pl.CostEstimate(flops=10**9, bytes_accessed=4 * 10**6, transcendentals=0),
        name="keep",
    )(plan, kv, kept)


def compressed_parts(stash, kv, seeds, plan, halves, axis):
    slots, tokens, width = stash.shape
    groups = 4
    tile = width // 16
    scale = PRIME * 2.0 / (PRIME - 1) * math.sqrt(3.0 / width)
    far = pl.BlockSpec(memory_space=pl.ANY)
    digits = jnp.asarray(row_digits(width))
    part = (R // halves, kv.shape[2])
    sides = (2, R // halves, slots * tokens)
    return pl.pallas_call(
        functools.partial(compress_kernel, tile, groups, scale, halves, axis),
        out_shape=[jax.ShapeDtypeStruct(sides, jnp.bfloat16), jax.ShapeDtypeStruct(part, jnp.bfloat16)],
        in_specs=[far] * 5,
        out_specs=[pl.BlockSpec(memory_space=pltpu.VMEM)] * 2,
        scratch_shapes=[
            pltpu.SMEM(seeds.shape, jnp.int32),
            pltpu.SMEM(plan.shape, jnp.int32),
            pltpu.VMEM((slots, tokens, width), jnp.bfloat16),
            pltpu.VMEM(kv.shape, jnp.bfloat16),
            pltpu.VMEM(digits.shape, jnp.bfloat16),
            pltpu.VMEM((2 * R, 128), jnp.bfloat16),
            pltpu.VMEM((2 * R, slots * tokens), jnp.float32),
            pltpu.SemaphoreType.DMA((2,)),
            pltpu.SemaphoreType.DMA((groups,)),
            pltpu.SemaphoreType.DMA((slots,)),
            pltpu.SemaphoreType.DMA,
        ],
        compiler_params=pltpu.CompilerParams(vmem_limit_bytes=60 * 2**20),
        cost_estimate=pl.CostEstimate(flops=8 * 10**9, bytes_accessed=28 * 10**6, transcendentals=0),
        name="compress",
    )(seeds, plan, stash, kv, digits)


def exchanged(value, axis, distance):
    size = lax.axis_size(axis)
    return lax.ppermute(value, axis, [(i, i ^ distance) for i in range(size)])


def split_kernel(axis, keep, got, *outs):
    chips = len(outs)
    rows = keep.shape[0] // chips
    chip = lax.axis_index(axis) // 2
    for step, out in enumerate(outs):
        at = pl.ds(pl.multiple_of((chip ^ step) * rows, rows), rows)
        out[...] = (keep[at, :] + got[at, :].astype(jnp.float32)).astype(out.dtype)


def sum_kernel(*refs):
    *terms, out = refs
    total = terms[0][...]
    for term in terms[1:]:
        total = total + term[...].astype(jnp.float32)
    out[...] = total.astype(out.dtype)


def assemble_kernel(axis, *refs):
    *pieces, out = refs
    chips = len(pieces) // 2
    rows = pieces[0].shape[0]
    device = lax.axis_index(axis)
    for side in range(2):
        core = lax.rem(device, 2) ^ side
        for step in range(chips):
            at = (core * chips + ((device // 2) ^ step)) * rows
            out[pl.ds(pl.multiple_of(at, rows), rows), :] = pieces[side * chips + step][...].astype(out.dtype)


def vmem_call(kernel, outs, name, *args, after=(), cost=None):
    inside, anywhere = pl.BlockSpec(memory_space=pltpu.VMEM), pl.BlockSpec(memory_space=pl.ANY)

    def body(*refs):
        kernel(*refs[:len(args)], *refs[len(args) + len(after):])

    return pl.pallas_call(
        body,
        out_shape=outs,
        in_specs=[inside] * len(args) + [anywhere] * len(after),
        out_specs=jax.tree.map(lambda _: inside, outs),
        compiler_params=pltpu.CompilerParams(vmem_limit_bytes=32 * 2**20),
        cost_estimate=cost,
        name=name,
    )(*args, *after)


def add_kernel(a, b, out):
    out[...] = (a[...].astype(jnp.float32) + b[...].astype(jnp.float32)).astype(out.dtype)


def add_after(a, b, *after):
    return vmem_call(add_kernel, jax.ShapeDtypeStruct(a.shape, a.dtype), "add", a, b, after=after)


def added(a, b):
    return (a.astype(jnp.float32) + b.astype(jnp.float32)).astype(jnp.bfloat16)


def between_places(value, swaps, axis, other_axis):
    size, others = lax.axis_size(axis), lax.axis_size(other_axis)
    goes = dict(swaps) | {b: a for a, b in swaps}
    pairs = [
        (i * size + place, i * size + goes[place] if place in goes else (i ^ 1) * size + place)
        for place in range(size)
        for i in range(others)
    ]
    return lax.ppermute(value, (other_axis, axis), pairs)


def chain(own, axis):
    size, mine = lax.axis_size(axis), lax.axis_index(axis)
    value = own
    for place in range(size - 1, 0, -1):
        got = lax.ppermute(value, axis, [(place, place - 1)])
        value = jnp.where(mine == place - 1, added(got, own), value)
    return value


def per_device(stashed, kv_grads, branch_grads, flora_seeds, plan):
    stash, kv, branch = stashed[0], kv_grads[0], branch_grads[0]
    size = lax.axis_size("dp")
    chips = size // 2
    columns = kv.shape[2]
    if size != 2 * chips or chips not in (1, 2, 4) or lax.axis_size("pipe") != 4:
        kept, _ = compressed_parts(stash, kv, flora_seeds, plan, 1, "dp")
        return lax.psum(kept_part(plan, kv, kept), "dp")[None], chain(branch, "pipe")[None]

    mine = lax.axis_index("pipe")
    rows = branch.shape[0] // 2
    first, second = branch[:rows], branch[rows:]
    pairwise, middle, across = ((3, 2), (1, 0)), ((2, 1),), ((2, 0),)

    def moved(value, swaps):
        return between_places(value, swaps, "pipe", "dp")

    first_a = moved(first, pairwise)
    second_a = moved(second, pairwise)
    kept, send = compressed_parts(stash, kv, flora_seeds, plan, 2, "dp")
    got = exchanged(send, "dp", 1)
    keep = kept_part(plan, kv, kept)
    first_2 = added(first_a, first)
    first_b = moved(first_2, middle)

    piece = (R // size, columns)
    own, *sends = vmem_call(
        functools.partial(split_kernel, "dp"),
        [jax.ShapeDtypeStruct(piece, jnp.float32 if s == 0 else jnp.bfloat16) for s in range(chips)],
        "split", keep, got,
    )
    gots = [exchanged(value, "dp", 2 * s) for s, value in enumerate(sends, 1)]

    second_2 = add_after(second_a, second, keep)
    second_b = moved(second_2, middle)
    second_d = moved(second_2, across)

    done = vmem_call(sum_kernel, jax.ShapeDtypeStruct(piece, jnp.bfloat16), "sum", own, *gots, )
    first_1 = add_after(first_b, first, done)
    first_c = moved(first_1, pairwise)
    here = [done] + [exchanged(done, "dp", 2 * s) for s in range(1, chips)]
    there = [exchanged(value, "dp", 1) for value in here]
    def by_place(values):
        out = values[3]
        for place in range(3):
            out = jnp.where(mine == place, values[place], out)
        return out

    running = jnp.concatenate([
        by_place([added(first_c, first), first_1, first_2, first]),
        by_place([added(added(second_d, second_a), second), added(second_b, second), second_2, second]),
    ])
    compressed = vmem_call(
        functools.partial(assemble_kernel, "dp"), jax.ShapeDtypeStruct((R, columns), jnp.float32),
        "assemble", *here, *there, after=[],
    )

    return compressed[None], running[None]


def solution(mesh):
    placed = (
        P("pipe", None, "dp", None),
        P("pipe", None, "dp", None),
        P("pipe", "dp", None),
        P("pipe", None),
        P("pipe", None),
    )
    return jax.shard_map(
        per_device,
        mesh=mesh,
        in_specs=placed,
        out_specs=(P("pipe", None, None), P("pipe", "dp", None)),
        check_vma=False,
    )
```

time: 63.1 us -> 40.2 us (0.64)
  starting transfers between devices: 29.2 us -> 17 us
  waiting for transfers between devices: 17.1 us -> 7.83 us
  other arithmetic: 5.5 us -> 1.24 us
  Pallas kernels: 9.16 us -> 11.3 us
  local copies, waits for them, and re-layouts: 1.06 us -> 1.92 us
    ppermute x8 -> x6, starting transfers between devices: 21.5 us -> 9.62 us  [between_places(): return lax.ppermute(value, (other_axis, axis), pairs)]
    ppermute x8 -> x6, waiting for transfers between devices: 8.25 us -> 0.02 us  [between_places(): return lax.ppermute(value, (other_axis, axis), pairs)]
    select_n x9 -> x1, other arithmetic: 4.67 us -> 0.34 us  [by_place(): out = jnp.where(mine == place, values[place], out)]
    pallas_call x3 -> x6, Pallas kernels: 1.65 us -> 3.32 us  [the longest x5 1.77 us: vmem_call(): pl.pallas_call(body, out_shape=outs, in_specs=[inside] * len(args) + [any...]
    slice x0 -> x1, local copies, waits for them, and re-layouts: none -> 1.07 us  [per_device(): first, second = (branch[:rows], branch[rows:])]
    ppermute x11, waiting for transfers between devices: 8.82 us -> 7.81 us  [exchanged(): return lax.ppermute(value, axis, [(i, i ^ distance) for i in range(size)])]
  transfers between devices with their start and end apart: 19 -> 17, of which waited for: 9 -> 4; matrix products, arithmetic and copies ran while one was open for 2% -> 3% of each run, Pallas kernels for 12% -> 25%
where the time goes in v2:
time: 40.2 us; the launch traced here: 40 us
  starting transfers between devices  17 us (42%)
  Pallas kernels  11.3 us (28%)
  waiting for transfers between devices  7.83 us (19%)
  local copies, waits for them, and re-layouts  1.92 us (5%)
  other arithmetic  1.24 us (3%)
  between operations  0.75 us (2%)
    ppermute x6, starting transfers between devices, between_places(): return lax.ppermute(value, (other_axis, axis), pairs)  9.62 us
    pallas_call x1, Pallas kernels, compressed_parts(): pl.pallas_call(functools.partial(compress_kernel, tile, groups, scale, ha...  7.96 us
    ppermute x11, waiting for transfers between devices, exchanged(): return lax.ppermute(value, axis, [(i, i ^ distance) for i in range(size)])  7.81 us
    ppermute x11, starting transfers between devices, exchanged(): return lax.ppermute(value, axis, [(i, i ^ distance) for i in range(size)])  7.36 us
    pallas_call x5, Pallas kernels, vmem_call(): pl.pallas_call(body, out_shape=outs, in_specs=[inside] * len(args) + [any...  1.77 us
    pallas_call x1, Pallas kernels, kept_part(): pl.pallas_call(keep_kernel, out_shape=jax.ShapeDtypeStruct((kept.shape[1]...  1.55 us
    slice x1, local copies, waits for them, and re-layouts, per_device(): first, second = (branch[:rows], branch[rows:])  1.07 us
    unnamed x8, local copies, waits for them, and re-layouts  0.85 us
  transfers between devices with their start and end apart: 17, of which 4 were waited for; matrix products, arithmetic and copies ran while one was open for 3% of the time, Pallas kernels for 25%

profile of v2, /device:TPU:0, one launch (start us, length us, event | category | flops | bytes accessed | tf_op | source)
XLA Modules:
  0.0 40.0 jit_solution(17928327069139891357)
XLA Ops:
  0.6 1.1 %slice_bitcast_fusion.1 = (bf16[16,8192]{1,0:T(8,128)(2,1)S(1)}, bf16[16,8192]{1,0:T(8,128)(2,1)S(1)}) fusion(bf16[1,32,8192]{2,1,0:T(8,128)(2,1)} %param.8), kind=kLoop, calls=%fused_computation.17 | loop fusion | bytes 1048576 | tf_op jit(solution)/shard_map/slice | solution.py:282
  1.7 3.1 %collective-permute-start.11 = (bf16[16,8192]{1,0:T(8,128)(2,1)S(1)}, bf16[16,8192]{1,0:T(8,128)(2,1)S(1)}, u32[]{:S(2)}, u32[]{:S(2)}) collective-permute-start(bf16[16,8192]{1,0:T(8,128)(2,1)S(1)} %get-tuple-element.16.refs_1_), channel_id=1, source_target_pairs={{0,1},{4,5},{8,9},{12,13},{16,17},{20,21},{24,25},{28,29},{1,0},{5... | collective-permute-start | bytes 786440 | tf_op jit(solution)/shard_map/ppermute | solution.py:259
  4.8 0.1 collective-permute-start.14
  4.9 8.0 %compress.1 = (bf16[2,128,128]{2,1,0:T(8,128)(2,1)}, bf16[128,2048]{1,0:T(8,128)(2,1)}) custom-call(s32[1,2]{1,0:T(1,128)} %seeds_hbm.1, s32[1,4]{1,0:T(1,128)} %plan_hbm.3, bf16[4,32,8192]{2,1,0:T(8,128)(2,1)} %bitcast.18, bf16[4,32,2048]{2,1,0:T(8,128)(2,1)} %bitcast.15, bf16[32,8192]{1,0:T(8,128)(2,1)} %constant.12.clone.digits_hbm), custom_call_target="tpu_custom_call" | custom-call | flops 8000000000 | bytes 28000000 | tf_op jit(solution)/shard_map/compress/pallas_call | solution.py:164
  12.8 0.1 collective-permute-start
  12.9 0.0 collective-permute-done.11
  12.9 0.1 fusion
  13.0 0.5 %collective-permute-start.12 = (bf16[16,8192]{1,0:T(8,128)(2,1)S(1)}, bf16[16,8192]{1,0:T(8,128)(2,1)S(1)}, u32[]{:S(2)}, u32[]{:S(2)}) collective-permute-start(bf16[16,8192]{1,0:T(8,128)(2,1)S(1)} %fusion), channel_id=1, source_target_pairs={{0,4},{4,0},{8,12},{12,8},{16,20},{20,16},{24,28},{28,24},{1,2},{5... | collective-permute-start | bytes 786440 | tf_op jit(solution)/shard_map/ppermute | solution.py:259
  13.6 0.8 %copy-done.2 = bf16[2,128,128]{2,1,0:T(8,128)(2,1)S(1)} copy-done((bf16[2,128,128]{2,1,0:T(8,128)(2,1)S(1)}, bf16[2,128,128]{2,1,0:T(8,128)(2,1)}, u32[]{:S(2)}) %copy-start.2) | copy-done | bytes 65560
  14.4 1.6 %keep.1.refs_0_.refs_2_ = f32[128,2048]{1,0:T(8,128)S(1)} custom-call(s32[1,4]{1,0:T(1,128)S(1)} %copy-done.1, bf16[4,32,2048]{2,1,0:T(8,128)(2,1)S(1)} %bitcast.16, bf16[2,128,128]{2,1,0:T(8,128)(2,1)S(1)} %copy-done.2), custom_call_target="tpu_custom_call" | custom-call | flops 1000000000 | bytes 4000000 | tf_op jit(solution)/shard_map/keep/pallas_call | solution.py:138
  16.0 0.1 split.1
  16.1 1.9 %collective-permute-start.1 = (bf16[32,2048]{1,0:T(8,128)(2,1)S(1)}, bf16[32,2048]{1,0:T(8,128)(2,1)S(1)}, u32[]{:S(2)}, u32[]{:S(2)}) collective-permute-start(bf16[32,2048]{1,0:T(8,128)(2,1)S(1)} %get-tuple-element.11), channel_id=1, source_target_pairs={{0,8},{4,12},{8,0},{12,4},{16,24},{20,28},{24,16},{28,20},{1,9},{5... | collective-permute-start | bytes 393224 | tf_op jit(solution)/shard_map/ppermute | solution.py:190
  18.0 1.5 %collective-permute-start.2 = (bf16[32,2048]{1,0:T(8,128)(2,1)S(1)}, bf16[32,2048]{1,0:T(8,128)(2,1)S(1)}, u32[]{:S(2)}, u32[]{:S(2)}) collective-permute-start(bf16[32,2048]{1,0:T(8,128)(2,1)S(1)} %get-tuple-element.12), channel_id=1, source_target_pairs={{0,16},{4,20},{8,24},{12,28},{16,0},{20,4},{24,8},{28,12},{1,17},{... | collective-permute-start | bytes 393224 | tf_op jit(solution)/shard_map/ppermute | solution.py:190
  19.5 0.1 collective-permute-start.3
  19.6 0.0 collective-permute-done.14.refs_0_
  19.6 0.1 add.52
  19.7 3.0 %collective-permute-start.16 = (bf16[16,8192]{1,0:T(8,128)(2,1)S(1)}, bf16[16,8192]{1,0:T(8,128)(2,1)S(1)}, u32[]{:S(2)}, u32[]{:S(2)}) collective-permute-start(bf16[16,8192]{1,0:T(8,128)(2,1)S(1)} %add.52), channel_id=1, source_target_pairs={{0,2},{4,6},{8,10},{12,14},{16,18},{20,22},{24,26},{28,30},{1,5},{... | collective-permute-start | bytes 786440 | tf_op jit(solution)/shard_map/ppermute | solution.py:259
  22.7 0.0 collective-permute-done.1.refs_1_
  22.7 3.3 %collective-permute-done.2.refs_2_ = bf16[32,2048]{1,0:T(8,128)(2,1)S(1)} collective-permute-done((bf16[32,2048]{1,0:T(8,128)(2,1)S(1)}, bf16[32,2048]{1,0:T(8,128)(2,1)S(1)}, u32[]{:S(2)}, u32[]{:S(2)}) %collective-permute-start.2) | collective-permute-done | bytes 131104 | tf_op jit(solution)/shard_map/ppermute | solution.py:190
  26.0 0.1 sum.1.refs_0_.refs_2_
  26.1 0.1 add.51
  26.1 2.9 %collective-permute-start.13 = (bf16[16,8192]{1,0:T(8,128)(2,1)S(1)}, bf16[16,8192]{1,0:T(8,128)(2,1)S(1)}, u32[]{:S(2)}, u32[]{:S(2)}) collective-permute-start(bf16[16,8192]{1,0:T(8,128)(2,1)S(1)} %add.51), channel_id=1, source_target_pairs={{0,1},{4,5},{8,9},{12,13},{16,17},{20,21},{24,25},{28,29},{1,0},{5... | collective-permute-start | bytes 786440 | tf_op jit(solution)/shard_map/ppermute | solution.py:259
  29.0 1.5 %collective-permute-start.6 = (bf16[32,2048]{1,0:T(8,128)(2,1)S(1)}, bf16[32,2048]{1,0:T(8,128)(2,1)S(1)}, u32[]{:S(2)}, u32[]{:S(2)}) collective-permute-start(bf16[32,2048]{1,0:T(8,128)(2,1)S(1)} %sum.1.refs_0_.refs_2_), channel_id=1, source_target_pairs={{0,24},{4,28},{8,16},{12,20},{16,8},{20,12},{24,0},{28,4},{1,25},{... | collective-permute-start | bytes 393224 | tf_op jit(solution)/shard_map/ppermute | solution.py:190
  30.5 1.2 %collective-permute-start.5 = (bf16[32,2048]{1,0:T(8,128)(2,1)S(1)}, bf16[32,2048]{1,0:T(8,128)(2,1)S(1)}, u32[]{:S(2)}, u32[]{:S(2)}) collective-permute-start(bf16[32,2048]{1,0:T(8,128)(2,1)S(1)} %sum.1.refs_0_.refs_2_), channel_id=1, source_target_pairs={{0,16},{4,20},{8,24},{12,28},{16,0},{20,4},{24,8},{28,12},{1,17},{... | collective-permute-start | bytes 393224 | tf_op jit(solution)/shard_map/ppermute | solution.py:190
  31.7 0.8 %collective-permute-start.4 = (bf16[32,2048]{1,0:T(8,128)(2,1)S(1)}, bf16[32,2048]{1,0:T(8,128)(2,1)S(1)}, u32[]{:S(2)}, u32[]{:S(2)}) collective-permute-start(bf16[32,2048]{1,0:T(8,128)(2,1)S(1)} %sum.1.refs_0_.refs_2_), channel_id=1, source_target_pairs={{0,8},{4,12},{8,0},{12,4},{16,24},{20,28},{24,16},{28,20},{1,9},{5... | collective-permute-start | bytes 393224 | tf_op jit(solution)/shard_map/ppermute | solution.py:190
  32.5 3.2 %collective-permute-done.6.refs_3_ = bf16[32,2048]{1,0:T(8,128)(2,1)S(1)} collective-permute-done((bf16[32,2048]{1,0:T(8,128)(2,1)S(1)}, bf16[32,2048]{1,0:T(8,128)(2,1)S(1)}, u32[]{:S(2)}, u32[]{:S(2)}) %collective-permute-start.6) | collective-permute-done | bytes 131104 | tf_op jit(solution)/shard_map/ppermute | solution.py:190
  35.7 1.1 %collective-permute-done.5.refs_2_ = bf16[32,2048]{1,0:T(8,128)(2,1)S(1)} collective-permute-done((bf16[32,2048]{1,0:T(8,128)(2,1)S(1)}, bf16[32,2048]{1,0:T(8,128)(2,1)S(1)}, u32[]{:S(2)}, u32[]{:S(2)}) %collective-permute-start.5) | collective-permute-done | bytes 131104 | tf_op jit(solution)/shard_map/ppermute | solution.py:190
  36.8 0.3 collective-permute-done.4.refs_1_
  37.1 0.2 collective-permute-start.8
  37.3 0.3 fusion.7
  37.7 0.8 %maximum_bitcast_fusion = bf16[1,32,8192]{2,1,0:T(8,128)(2,1)} fusion(bf16[16,8192]{1,0:T(8,128)(2,1)S(1)} %get-tuple-element.15, bf16[16,8192]{1,0:T(8,128)(2,1)S(1)} %get-tuple-element.14), kind=kLoop, calls=%fused_computation.8 | loop fusion | flops 1048576 | bytes 1048576 | tf_op jit(solution)/shard_map/broadcast_in_dim | solution.py:328
  38.5 1.5 %assemble.1 = f32[256,2048]{1,0:T(8,128)} custom-call(bf16[32,2048]{1,0:T(8,128)(2,1)S(1)} %sum.1.refs_0_.refs_2_, bf16[32,2048]{1,0:T(8,128)(2,1)S(1)} %collective-permute-done.4.refs_1_, bf16[32,2048]{1,0:T(8,128)(2,1)S(1)} %collective-permute-done.5.refs_2_, bf16[32,2048]{1,0:T(8,128)(2,1)S(1)} %collective-permute-done.6.refs_3_, ...), custom_call_target="tpu_custom_call" | custom-call | tf_op jit(solution)/shard_map/assemble/pallas_call | solution.py:228
  (21 shorter events, 0.0 us)
Async XLA Ops:
  1.7 11.2 %collective-permute-start.11 = (bf16[16,8192]{1,0:T(8,128)(2,1)S(1)}, bf16[16,8192]{1,0:T(8,128)(2,1)S(1)}, u32[]{:S(2)}, u32[]{:S(2)}) collective-permute-start(bf16[16,8192]{1,0:T(8,128)(2,1)S(1)} %get-tuple-element.16.refs_1_), channel_id=1, source_target_pairs={{0,1},{4,5},{8,9},{12,13},{16,17},{20,21},{24,25},{28,29},{1,0},{5... | collective-permute-start | bytes 786440 | tf_op jit(solution)/shard_map/ppermute | solution.py:259
  4.8 14.9 %collective-permute-start.14 = (bf16[16,8192]{1,0:T(8,128)(2,1)S(1)}, bf16[16,8192]{1,0:T(8,128)(2,1)S(1)}, u32[]{:S(2)}, u32[]{:S(2)}) collective-permute-start(bf16[16,8192]{1,0:T(8,128)(2,1)S(1)} %get-tuple-element.17.refs_1_), channel_id=1, source_target_pairs={{0,1},{4,5},{8,9},{12,13},{16,17},{20,21},{24,25},{28,29},{1,0},{5... | collective-permute-start | bytes 786440 | tf_op jit(solution)/shard_map/ppermute | solution.py:259
  4.9 8.1 %copy-start.3 = (bf16[1,32,8192]{2,1,0:T(8,128)(2,1)S(1)}, bf16[1,32,8192]{2,1,0:T(8,128)(2,1)}, u32[]{:S(2)}) copy-start(bf16[1,32,8192]{2,1,0:T(8,128)(2,1)} %param.8) | copy-start | bytes 1572868
  4.9 8.7 %copy-start = (bf16[1,4,32,2048]{3,2,1,0:T(8,128)(2,1)S(1)}, bf16[1,4,32,2048]{3,2,1,0:T(8,128)(2,1)}, u32[]{:S(2)}) copy-start(bf16[1,4,32,2048]{3,2,1,0:T(8,128)(2,1)} %param.7) | copy-start | bytes 1572868
  4.9 8.7 %copy-start.1 = (s32[1,4]{1,0:T(1,128)S(1)}, s32[1,4]{1,0:T(1,128)}, u32[]{:S(2)}) copy-start(s32[1,4]{1,0:T(1,128)} %plan_hbm.3) | copy-start | bytes 52
  12.8 3.1 %collective-permute-start = (bf16[128,2048]{1,0:T(8,128)(2,1)}, bf16[128,2048]{1,0:T(8,128)(2,1)S(1)}, u32[]{:S(2)}, u32[]{:S(2)}) collective-permute-start(bf16[128,2048]{1,0:T(8,128)(2,1)} %get-tuple-element.9), channel_id=1, source_target_pairs={{0,4},{4,0},{8,12},{12,8},{16,20},{20,16},{24,28},{28,24},{1,5},{5... | collective-permute-start | bytes 1572872 | tf_op jit(solution)/shard_map/ppermute | solution.py:190
  13.0 13.0 %collective-permute-start.12 = (bf16[16,8192]{1,0:T(8,128)(2,1)S(1)}, bf16[16,8192]{1,0:T(8,128)(2,1)S(1)}, u32[]{:S(2)}, u32[]{:S(2)}) collective-permute-start(bf16[16,8192]{1,0:T(8,128)(2,1)S(1)} %fusion), channel_id=1, source_target_pairs={{0,4},{4,0},{8,12},{12,8},{16,20},{20,16},{24,28},{28,24},{1,2},{5... | collective-permute-start | bytes 786440 | tf_op jit(solution)/shard_map/ppermute | solution.py:259
  13.6 0.8 %copy-start.2 = (bf16[2,128,128]{2,1,0:T(8,128)(2,1)S(1)}, bf16[2,128,128]{2,1,0:T(8,128)(2,1)}, u32[]{:S(2)}) copy-start(bf16[2,128,128]{2,1,0:T(8,128)(2,1)} %get-tuple-element.8.kept) | copy-start | bytes 196612
  16.1 6.6 %collective-permute-start.1 = (bf16[32,2048]{1,0:T(8,128)(2,1)S(1)}, bf16[32,2048]{1,0:T(8,128)(2,1)S(1)}, u32[]{:S(2)}, u32[]{:S(2)}) collective-permute-start(bf16[32,2048]{1,0:T(8,128)(2,1)S(1)} %get-tuple-element.11), channel_id=1, source_target_pairs={{0,8},{4,12},{8,0},{12,4},{16,24},{20,28},{24,16},{28,20},{1,9},{5... | collective-permute-start | bytes 393224 | tf_op jit(solution)/shard_map/ppermute | solution.py:190
  18.0 8.0 %collective-permute-start.2 = (bf16[32,2048]{1,0:T(8,128)(2,1)S(1)}, bf16[32,2048]{1,0:T(8,128)(2,1)S(1)}, u32[]{:S(2)}, u32[]{:S(2)}) collective-permute-start(bf16[32,2048]{1,0:T(8,128)(2,1)S(1)} %get-tuple-element.12), channel_id=1, source_target_pairs={{0,16},{4,20},{8,24},{12,28},{16,0},{20,4},{24,8},{28,12},{1,17},{... | collective-permute-start | bytes 393224 | tf_op jit(solution)/shard_map/ppermute | solution.py:190
  19.5 6.4 %collective-permute-start.3 = (bf16[32,2048]{1,0:T(8,128)(2,1)S(1)}, bf16[32,2048]{1,0:T(8,128)(2,1)S(1)}, u32[]{:S(2)}, u32[]{:S(2)}) collective-permute-start(bf16[32,2048]{1,0:T(8,128)(2,1)S(1)} %get-tuple-element.13), channel_id=1, source_target_pairs={{0,24},{4,28},{8,16},{12,20},{16,8},{20,12},{24,0},{28,4},{1,25},{... | collective-permute-start | bytes 393224 | tf_op jit(solution)/shard_map/ppermute | solution.py:190
  19.7 12.0 %collective-permute-start.16 = (bf16[16,8192]{1,0:T(8,128)(2,1)S(1)}, bf16[16,8192]{1,0:T(8,128)(2,1)S(1)}, u32[]{:S(2)}, u32[]{:S(2)}) collective-permute-start(bf16[16,8192]{1,0:T(8,128)(2,1)S(1)} %add.52), channel_id=1, source_target_pairs={{0,2},{4,6},{8,10},{12,14},{16,18},{20,22},{24,26},{28,30},{1,5},{... | collective-permute-start | bytes 786440 | tf_op jit(solution)/shard_map/ppermute | solution.py:259
  22.7 9.8 %collective-permute-start.15 = (bf16[16,8192]{1,0:T(8,128)(2,1)S(1)}, bf16[16,8192]{1,0:T(8,128)(2,1)S(1)}, u32[]{:S(2)}, u32[]{:S(2)}) collective-permute-start(bf16[16,8192]{1,0:T(8,128)(2,1)S(1)} %add.52), channel_id=1, source_target_pairs={{0,4},{4,0},{8,12},{12,8},{16,20},{20,16},{24,28},{28,24},{1,2},{5... | collective-permute-start | bytes 786440 | tf_op jit(solution)/shard_map/ppermute | solution.py:259
  26.1 11.2 %collective-permute-start.13 = (bf16[16,8192]{1,0:T(8,128)(2,1)S(1)}, bf16[16,8192]{1,0:T(8,128)(2,1)S(1)}, u32[]{:S(2)}, u32[]{:S(2)}) collective-permute-start(bf16[16,8192]{1,0:T(8,128)(2,1)S(1)} %add.51), channel_id=1, source_target_pairs={{0,1},{4,5},{8,9},{12,13},{16,17},{20,21},{24,25},{28,29},{1,0},{5... | collective-permute-start | bytes 786440 | tf_op jit(solution)/shard_map/ppermute | solution.py:259
  29.0 6.7 %collective-permute-start.6 = (bf16[32,2048]{1,0:T(8,128)(2,1)S(1)}, bf16[32,2048]{1,0:T(8,128)(2,1)S(1)}, u32[]{:S(2)}, u32[]{:S(2)}) collective-permute-start(bf16[32,2048]{1,0:T(8,128)(2,1)S(1)} %sum.1.refs_0_.refs_2_), channel_id=1, source_target_pairs={{0,24},{4,28},{8,16},{12,20},{16,8},{20,12},{24,0},{28,4},{1,25},{... | collective-permute-start | bytes 393224 | tf_op jit(solution)/shard_map/ppermute | solution.py:190
  30.5 6.3 %collective-permute-start.5 = (bf16[32,2048]{1,0:T(8,128)(2,1)S(1)}, bf16[32,2048]{1,0:T(8,128)(2,1)S(1)}, u32[]{:S(2)}, u32[]{:S(2)}) collective-permute-start(bf16[32,2048]{1,0:T(8,128)(2,1)S(1)} %sum.1.refs_0_.refs_2_), channel_id=1, source_target_pairs={{0,16},{4,20},{8,24},{12,28},{16,0},{20,4},{24,8},{28,12},{1,17},{... | collective-permute-start | bytes 393224 | tf_op jit(solution)/shard_map/ppermute | solution.py:190
  31.7 5.3 %collective-permute-start.4 = (bf16[32,2048]{1,0:T(8,128)(2,1)S(1)}, bf16[32,2048]{1,0:T(8,128)(2,1)S(1)}, u32[]{:S(2)}, u32[]{:S(2)}) collective-permute-start(bf16[32,2048]{1,0:T(8,128)(2,1)S(1)} %sum.1.refs_0_.refs_2_), channel_id=1, source_target_pairs={{0,8},{4,12},{8,0},{12,4},{16,24},{20,28},{24,16},{28,20},{1,9},{5... | collective-permute-start | bytes 393224 | tf_op jit(solution)/shard_map/ppermute | solution.py:190
  32.5 6.0 %collective-permute-start.7 = (bf16[32,2048]{1,0:T(8,128)(2,1)S(1)}, bf16[32,2048]{1,0:T(8,128)(2,1)S(1)}, u32[]{:S(2)}, u32[]{:S(2)}) collective-permute-start(bf16[32,2048]{1,0:T(8,128)(2,1)S(1)} %sum.1.refs_0_.refs_2_), channel_id=1, source_target_pairs={{0,4},{4,0},{8,12},{12,8},{16,20},{20,16},{24,28},{28,24},{1,5},{5... | collective-permute-start | bytes 393224 | tf_op jit(solution)/shard_map/ppermute | solution.py:190
  35.7 2.8 %collective-permute-start.10 = (bf16[32,2048]{1,0:T(8,128)(2,1)S(1)}, bf16[32,2048]{1,0:T(8,128)(2,1)S(1)}, u32[]{:S(2)}, u32[]{:S(2)}) collective-permute-start(bf16[32,2048]{1,0:T(8,128)(2,1)S(1)} %collective-permute-done.6.refs_3_), channel_id=1, source_target_pairs={{0,4},{4,0},{8,12},{12,8},{16,20},{20,16},{24,28},{28,24},{1,5},{5... | collective-permute-start | bytes 393224 | tf_op jit(solution)/shard_map/ppermute | solution.py:190
  36.8 1.7 %collective-permute-start.9 = (bf16[32,2048]{1,0:T(8,128)(2,1)S(1)}, bf16[32,2048]{1,0:T(8,128)(2,1)S(1)}, u32[]{:S(2)}, u32[]{:S(2)}) collective-permute-start(bf16[32,2048]{1,0:T(8,128)(2,1)S(1)} %collective-permute-done.5.refs_2_), channel_id=1, source_target_pairs={{0,4},{4,0},{8,12},{12,8},{16,20},{20,16},{24,28},{28,24},{1,5},{5... | collective-permute-start | bytes 393224 | tf_op jit(solution)/shard_map/ppermute | solution.py:190
  37.1 1.4 %collective-permute-start.8 = (bf16[32,2048]{1,0:T(8,128)(2,1)S(1)}, bf16[32,2048]{1,0:T(8,128)(2,1)S(1)}, u32[]{:S(2)}, u32[]{:S(2)}) collective-permute-start(bf16[32,2048]{1,0:T(8,128)(2,1)S(1)} %collective-permute-done.4.refs_1_), channel_id=1, source_target_pairs={{0,4},{4,0},{8,12},{12,8},{16,20},{20,16},{24,28},{28,24},{1,5},{5... | collective-permute-start | bytes 393224 | tf_op jit(solution)/shard_map/ppermute | solution.py:190

commit v3 on v2

--- a/solution.py
+++ b/solution.py
@@ -56,6 +56,10 @@
     digit = jnp.where((term & 1) == 0, high, whole - high)
     digit = jnp.where(term >= 20, jnp.where(term < 22, 1.0, 0.0), digit)
     return digit.astype(jnp.bfloat16)
+
+
+def tokens_dot(left, right):
+    return lax.dot_general(left, right, (((0,), (0,)), ((), ())), preferred_element_type=jnp.float32)
 
 
 def compress_kernel(
@@ -76,15 +80,11 @@
         )
         for g in range(groups)
     ]
-    for copy in (*scalars, digit_copy, *copies):
+    kv_copy = pltpu.make_async_copy(kv_hbm, kv, kv_sem)
+    for copy in (*scalars, digit_copy, *copies, kv_copy):
         copy.start()
     for copy in scalars:
         copy.wait()
-    kv_copies = [
-        pltpu.make_async_copy(kv_hbm.at[plan[0, k]], kv.at[k], kv_sem.at[k]) for k in range(slots)
-    ]
-    for copy in kv_copies:
-        copy.start()
     columns[0:R, :] = column_digits(seeds[0, 0], R)
     columns[R:, :] = column_digits(seeds[0, 1], R)
     digit_copy.wait()
@@ -97,70 +97,53 @@
             turns = hashed * jnp.float32(1 / PRIME)
             proj = ((turns - jnp.round(turns)) * jnp.float32(scale)).astype(jnp.bfloat16)
             total[...] += lax.dot_general(
-                proj, x[:, :, part].reshape(slots * tokens, tile), (((1,), (1,)), ((), ())),
+                x[:, :, part].reshape(slots * tokens, tile), proj, (((1,), (1,)), ((), ())),
                 preferred_element_type=jnp.float32,
             )
-    for copy in kv_copies:
-        copy.wait()
+    count = slots * tokens
+    slot_row = lax.broadcasted_iota(jnp.int32, (count, count), 0)
+    place = slot_row
+    for k in range(slots):
+        within = (slot_row >= k * tokens) & (slot_row < (k + 1) * tokens)
+        place = jnp.where(within, slot_row + (plan[0, k] - k) * tokens, place)
+    moves = (place == lax.broadcasted_iota(jnp.int32, (count, count), 1)).astype(jnp.bfloat16)
+    total[...] = tokens_dot(moves, total[...].astype(jnp.bfloat16))
+    kv_copy.wait()
     half = kv.shape[2] // 2
     targets = kv[...].reshape(slots * tokens, 2 * half)
     rows = R // halves
     mine = lax.rem(lax.axis_index(axis), halves)
     for side in range(2):
-        kept[side] = total[pl.ds(pl.multiple_of(side * R + mine * rows, rows), rows), :].astype(jnp.bfloat16)
+        kept[side] = total[:, pl.ds(pl.multiple_of(side * R + mine * rows, rows), rows)].astype(jnp.bfloat16)
         if halves > 1:
             other = pl.multiple_of(side * R + (1 - mine) * rows, rows)
-            left = total[pl.ds(other, rows), :].astype(jnp.bfloat16)
+            left = total[:, pl.ds(other, rows)].astype(jnp.bfloat16)
             cols = slice(side * half, (side + 1) * half)
-            send[:, cols] = jnp.dot(
-                left, targets[:, cols], preferred_element_type=jnp.float32
-            ).astype(send.dtype)
-
-
-def keep_kernel(plan_hbm, kv_hbm, kept, out, plan, kv, plan_sem, kv_sem):
+            send[:, cols] = tokens_dot(left, targets[:, cols]).astype(send.dtype)
+
+
+def keep_kernel(kept, kv, out):
     slots, tokens, width = kv.shape
-    plan_copy = pltpu.make_async_copy(plan_hbm, plan, plan_sem)
-    plan_copy.start()
-    plan_copy.wait()
-    copies = [pltpu.make_async_copy(kv_hbm.at[plan[0, k]], kv.at[k], kv_sem.at[k]) for k in range(slots)]
-    for copy in copies:
-        copy.start()
-    for copy in copies:
-        copy.wait()
     targets = kv[...].reshape(slots * tokens, width)
     for side in range(2):
         cols = slice(side * width // 2, (side + 1) * width // 2)
-        out[:, cols] = jnp.dot(kept[side], targets[:, cols], preferred_element_type=jnp.float32)
-
-
-def kept_part(plan, kv, kept):
-    inside, far = pl.BlockSpec(memory_space=pltpu.VMEM), pl.BlockSpec(memory_space=pl.ANY)
-    return pl.pallas_call(
-        keep_kernel,
-        out_shape=jax.ShapeDtypeStruct((kept.shape[1], kv.shape[2]), jnp.float32),
-        in_specs=[far, far, inside],
-        out_specs=inside,
-        scratch_shapes=[
-            pltpu.SMEM(plan.shape, jnp.int32),
-            pltpu.VMEM(kv.shape, jnp.bfloat16),
-            pltpu.SemaphoreType.DMA,
-            pltpu.SemaphoreType.DMA((kv.shape[0],)),
-        ],
-        compiler_params=pltpu.CompilerParams(vmem_limit_bytes=16 * 2**20),
-        cost_estimate=pl.CostEstimate(flops=10**9, bytes_accessed=4 * 10**6, transcendentals=0),
-        name="keep",
-    )(plan, kv, kept)
+        out[:, cols] = tokens_dot(kept[side], targets[:, cols])
+
+
+def kept_part(kept, kv):
+    out = jax.ShapeDtypeStruct((kept.shape[2], kv.shape[2]), jnp.float32)
+    return vmem_call(keep_kernel, out, "keep", kept, kv)
 
 
 def compressed_parts(stash, kv, seeds, plan, halves, axis):
     slots, tokens, width = stash.shape
-    groups = 4
-    tile = width // 16
+    groups = 2
+    tile = width // 8
     scale = PRIME * 2.0 / (PRIME - 1) * math.sqrt(3.0 / width)
     far = pl.BlockSpec(memory_space=pl.ANY)
     digits = jnp.asarray(row_digits(width))
     part = (R // halves, kv.shape[2])
-    sides = (2, R // halves, slots * tokens)
+    sides = (2, slots * tokens, R // halves)
     return pl.pallas_call(
         functools.partial(compress_kernel, tile, groups, scale, halves, axis),
         out_shape=[jax.ShapeDtypeStruct(sides, jnp.bfloat16), jax.ShapeDtypeStruct(part, jnp.bfloat16)],
@@ -173,10 +156,10 @@
             pltpu.VMEM(kv.shape, jnp.bfloat16),
             pltpu.VMEM(digits.shape, jnp.bfloat16),
             pltpu.VMEM((2 * R, 128), jnp.bfloat16),
-            pltpu.VMEM((2 * R, slots * tokens), jnp.float32),
+            pltpu.VMEM((slots * tokens, 2 * R), jnp.float32),
             pltpu.SemaphoreType.DMA((2,)),
             pltpu.SemaphoreType.DMA((groups,)),
-            pltpu.SemaphoreType.DMA((slots,)),
+            pltpu.SemaphoreType.DMA,
             pltpu.SemaphoreType.DMA,
         ],
         compiler_params=pltpu.CompilerParams(vmem_limit_bytes=60 * 2**20),
@@ -275,7 +258,7 @@
     columns = kv.shape[2]
     if size != 2 * chips or chips not in (1, 2, 4) or lax.axis_size("pipe") != 4:
         kept, _ = compressed_parts(stash, kv, flora_seeds, plan, 1, "dp")
-        return lax.psum(kept_part(plan, kv, kept), "dp")[None], chain(branch, "pipe")[None]
+        return lax.psum(kept_part(kept, kv), "dp")[None], chain(branch, "pipe")[None]
 
     mine = lax.axis_index("pipe")
     rows = branch.shape[0] // 2
@@ -289,7 +272,7 @@
     second_a = moved(second, pairwise)
     kept, send = compressed_parts(stash, kv, flora_seeds, plan, 2, "dp")
     got = exchanged(send, "dp", 1)
-    keep = kept_part(plan, kv, kept)
+    keep = kept_part(kept, kv)
     first_2 = added(first_a, first)
     first_b = moved(first_2, middle)
 

time: 40.2 us -> 38.5 us (0.958)
  Pallas kernels: 11.3 us -> 9.55 us
    pallas_call x1 -> x0, Pallas kernels: 1.55 us -> none  [kept_part(): pl.pallas_call(keep_kernel, out_shape=jax.ShapeDtypeStruct((kept.shape[1]...]
    pallas_call x1, Pallas kernels: 7.96 us -> 7.49 us  [compressed_parts(): pl.pallas_call(functools.partial(compress_kernel, tile, groups, scale, ha...]
    pallas_call x5 -> x6, Pallas kernels: 1.77 us -> 2.07 us  [vmem_call(): pl.pallas_call(body, out_shape=outs, in_specs=[inside] * len(args) + [any...]
    unnamed x8 -> x6, local copies, waits for them, and re-layouts: 0.85 us -> 0.85 us
  transfers between devices with their start and end apart: 17 -> 17, of which waited for: 4 -> 5; matrix products, arithmetic and copies ran while one was open for 3% -> 3% of each run, Pallas kernels for 25% -> 21%
where the time goes in v3:
time: 38.5 us; the launch traced here: 38.3 us
  starting transfers between devices  16.6 us (43%)
  Pallas kernels  9.55 us (25%)
  waiting for transfers between devices  8.21 us (21%)
  local copies, waits for them, and re-layouts  1.91 us (5%)
  other arithmetic  1.24 us (3%)
  between operations  0.73 us (2%)
    ppermute x6, starting transfers between devices, between_places(): return lax.ppermute(value, (other_axis, axis), pairs)  9.27 us
    ppermute x11, waiting for transfers between devices, exchanged(): return lax.ppermute(value, axis, [(i, i ^ distance) for i in range(size)])  8.19 us
    pallas_call x1, Pallas kernels, compressed_parts(): pl.pallas_call(functools.partial(compress_kernel, tile, groups, scale, ha...  7.49 us
    ppermute x11, starting transfers between devices, exchanged(): return lax.ppermute(value, axis, [(i, i ^ distance) for i in range(size)])  7.37 us
    pallas_call x6, Pallas kernels, vmem_call(): pl.pallas_call(body, out_shape=outs, in_specs=[inside] * len(args) + [any...  2.07 us
    slice x1, local copies, waits for them, and re-layouts, per_device(): first, second = (branch[:rows], branch[rows:])  1.07 us
    unnamed x6, local copies, waits for them, and re-layouts  0.85 us
    broadcast_in_dim x1, other arithmetic, per_device(): return (compressed[None], running[None])  0.83 us
  transfers between devices with their start and end apart: 17, of which 5 were waited for; matrix products, arithmetic and copies ran while one was open for 3% of the time, Pallas kernels for 21%

profile of v3, /device:TPU:0, one launch (start us, length us, event | category | flops | bytes accessed | tf_op | source)
XLA Modules:
  0.0 38.3 jit_solution(16171261715073546871)
XLA Ops:
  0.6 1.1 %slice_bitcast_fusion.1 = (bf16[16,8192]{1,0:T(8,128)(2,1)S(1)}, bf16[16,8192]{1,0:T(8,128)(2,1)S(1)}) fusion(bf16[1,32,8192]{2,1,0:T(8,128)(2,1)} %param.8), kind=kLoop, calls=%fused_computation.17 | loop fusion | bytes 1048576 | tf_op jit(solution)/shard_map/slice | solution.py:265
  1.7 3.1 %collective-permute-start.11 = (bf16[16,8192]{1,0:T(8,128)(2,1)S(1)}, bf16[16,8192]{1,0:T(8,128)(2,1)S(1)}, u32[]{:S(2)}, u32[]{:S(2)}) collective-permute-start(bf16[16,8192]{1,0:T(8,128)(2,1)S(1)} %get-tuple-element.16.refs_1_), channel_id=1, source_target_pairs={{0,1},{4,5},{8,9},{12,13},{16,17},{20,21},{24,25},{28,29},{1,0},{5... | collective-permute-start | bytes 786440 | tf_op jit(solution)/shard_map/ppermute | solution.py:242
  4.8 0.1 collective-permute-start.14
  4.9 7.5 %compress.1 = (bf16[2,128,128]{2,1,0:T(8,128)(2,1)}, bf16[128,2048]{1,0:T(8,128)(2,1)}) custom-call(s32[1,2]{1,0:T(1,128)} %seeds_hbm.1, s32[1,4]{1,0:T(1,128)} %plan_hbm.1, bf16[4,32,8192]{2,1,0:T(8,128)(2,1)} %bitcast.18, bf16[4,32,2048]{2,1,0:T(8,128)(2,1)} %bitcast.15, bf16[32,8192]{1,0:T(8,128)(2,1)} %constant.12.clone.digits_hbm), custom_call_target="tpu_custom_call" | custom-call | flops 8000000000 | bytes 28000000 | tf_op jit(solution)/shard_map/compress/pallas_call | solution.py:147
  12.4 0.1 collective-permute-start
  12.4 0.0 collective-permute-done.11
  12.5 0.1 fusion
  12.5 0.5 %collective-permute-start.12 = (bf16[16,8192]{1,0:T(8,128)(2,1)S(1)}, bf16[16,8192]{1,0:T(8,128)(2,1)S(1)}, u32[]{:S(2)}, u32[]{:S(2)}) collective-permute-start(bf16[16,8192]{1,0:T(8,128)(2,1)S(1)} %fusion), channel_id=1, source_target_pairs={{0,4},{4,0},{8,12},{12,8},{16,20},{20,16},{24,28},{28,24},{1,2},{5... | collective-permute-start | bytes 786440 | tf_op jit(solution)/shard_map/ppermute | solution.py:242
  13.1 0.8 %copy-done.1 = bf16[2,128,128]{2,1,0:T(8,128)(2,1)S(1)} copy-done((bf16[2,128,128]{2,1,0:T(8,128)(2,1)S(1)}, bf16[2,128,128]{2,1,0:T(8,128)(2,1)}, u32[]{:S(2)}) %copy-start.1) | copy-done | bytes 65560
  13.9 0.3 keep.1.refs_0_.refs_2_
  14.2 0.3 collective-permute-done.refs_1_
  14.6 0.1 split.1
  14.6 1.9 %collective-permute-start.1 = (bf16[32,2048]{1,0:T(8,128)(2,1)S(1)}, bf16[32,2048]{1,0:T(8,128)(2,1)S(1)}, u32[]{:S(2)}, u32[]{:S(2)}) collective-permute-start(bf16[32,2048]{1,0:T(8,128)(2,1)S(1)} %get-tuple-element.11), channel_id=1, source_target_pairs={{0,8},{4,12},{8,0},{12,4},{16,24},{20,28},{24,16},{28,20},{1,9},{5... | collective-permute-start | bytes 393224 | tf_op jit(solution)/shard_map/ppermute | solution.py:173
  16.6 1.5 %collective-permute-start.2 = (bf16[32,2048]{1,0:T(8,128)(2,1)S(1)}, bf16[32,2048]{1,0:T(8,128)(2,1)S(1)}, u32[]{:S(2)}, u32[]{:S(2)}) collective-permute-start(bf16[32,2048]{1,0:T(8,128)(2,1)S(1)} %get-tuple-element.12), channel_id=1, source_target_pairs={{0,16},{4,20},{8,24},{12,28},{16,0},{20,4},{24,8},{28,12},{1,17},{... | collective-permute-start | bytes 393224 | tf_op jit(solution)/shard_map/ppermute | solution.py:173
  18.1 0.1 collective-permute-start.3
  18.2 0.0 collective-permute-done.14.refs_0_
  18.2 0.1 add.52
  18.3 3.0 %collective-permute-start.16 = (bf16[16,8192]{1,0:T(8,128)(2,1)S(1)}, bf16[16,8192]{1,0:T(8,128)(2,1)S(1)}, u32[]{:S(2)}, u32[]{:S(2)}) collective-permute-start(bf16[16,8192]{1,0:T(8,128)(2,1)S(1)} %add.52), channel_id=1, source_target_pairs={{0,2},{4,6},{8,10},{12,14},{16,18},{20,22},{24,26},{28,30},{1,5},{... | collective-permute-start | bytes 786440 | tf_op jit(solution)/shard_map/ppermute | solution.py:242
  21.3 3.3 %collective-permute-done.2.refs_2_ = bf16[32,2048]{1,0:T(8,128)(2,1)S(1)} collective-permute-done((bf16[32,2048]{1,0:T(8,128)(2,1)S(1)}, bf16[32,2048]{1,0:T(8,128)(2,1)S(1)}, u32[]{:S(2)}, u32[]{:S(2)}) %collective-permute-start.2) | collective-permute-done | bytes 131104 | tf_op jit(solution)/shard_map/ppermute | solution.py:173
  24.6 0.1 sum.1.refs_0_.refs_2_
  24.7 0.1 add.51
  24.8 2.5 %collective-permute-start.13 = (bf16[16,8192]{1,0:T(8,128)(2,1)S(1)}, bf16[16,8192]{1,0:T(8,128)(2,1)S(1)}, u32[]{:S(2)}, u32[]{:S(2)}) collective-permute-start(bf16[16,8192]{1,0:T(8,128)(2,1)S(1)} %add.51), channel_id=1, source_target_pairs={{0,1},{4,5},{8,9},{12,13},{16,17},{20,21},{24,25},{28,29},{1,0},{5... | collective-permute-start | bytes 786440 | tf_op jit(solution)/shard_map/ppermute | solution.py:242
  27.3 1.5 %collective-permute-start.6 = (bf16[32,2048]{1,0:T(8,128)(2,1)S(1)}, bf16[32,2048]{1,0:T(8,128)(2,1)S(1)}, u32[]{:S(2)}, u32[]{:S(2)}) collective-permute-start(bf16[32,2048]{1,0:T(8,128)(2,1)S(1)} %sum.1.refs_0_.refs_2_), channel_id=1, source_target_pairs={{0,24},{4,28},{8,16},{12,20},{16,8},{20,12},{24,0},{28,4},{1,25},{... | collective-permute-start | bytes 393224 | tf_op jit(solution)/shard_map/ppermute | solution.py:173
  28.8 1.2 %collective-permute-start.5 = (bf16[32,2048]{1,0:T(8,128)(2,1)S(1)}, bf16[32,2048]{1,0:T(8,128)(2,1)S(1)}, u32[]{:S(2)}, u32[]{:S(2)}) collective-permute-start(bf16[32,2048]{1,0:T(8,128)(2,1)S(1)} %sum.1.refs_0_.refs_2_), channel_id=1, source_target_pairs={{0,16},{4,20},{8,24},{12,28},{16,0},{20,4},{24,8},{28,12},{1,17},{... | collective-permute-start | bytes 393224 | tf_op jit(solution)/shard_map/ppermute | solution.py:173
  30.0 0.8 %collective-permute-start.4 = (bf16[32,2048]{1,0:T(8,128)(2,1)S(1)}, bf16[32,2048]{1,0:T(8,128)(2,1)S(1)}, u32[]{:S(2)}, u32[]{:S(2)}) collective-permute-start(bf16[32,2048]{1,0:T(8,128)(2,1)S(1)} %sum.1.refs_0_.refs_2_), channel_id=1, source_target_pairs={{0,8},{4,12},{8,0},{12,4},{16,24},{20,28},{24,16},{28,20},{1,9},{5... | collective-permute-start | bytes 393224 | tf_op jit(solution)/shard_map/ppermute | solution.py:173
  30.8 3.4 %collective-permute-done.6.refs_3_ = bf16[32,2048]{1,0:T(8,128)(2,1)S(1)} collective-permute-done((bf16[32,2048]{1,0:T(8,128)(2,1)S(1)}, bf16[32,2048]{1,0:T(8,128)(2,1)S(1)}, u32[]{:S(2)}, u32[]{:S(2)}) %collective-permute-start.6) | collective-permute-done | bytes 131104 | tf_op jit(solution)/shard_map/ppermute | solution.py:173
  34.2 0.8 %collective-permute-done.5.refs_2_ = bf16[32,2048]{1,0:T(8,128)(2,1)S(1)} collective-permute-done((bf16[32,2048]{1,0:T(8,128)(2,1)S(1)}, bf16[32,2048]{1,0:T(8,128)(2,1)S(1)}, u32[]{:S(2)}, u32[]{:S(2)}) %collective-permute-start.5) | collective-permute-done | bytes 131104 | tf_op jit(solution)/shard_map/ppermute | solution.py:173
  35.1 0.3 collective-permute-done.4.refs_1_
  35.4 0.2 collective-permute-start.8
  35.6 0.3 fusion.7
  35.9 0.8 %maximum_bitcast_fusion = bf16[1,32,8192]{2,1,0:T(8,128)(2,1)} fusion(bf16[16,8192]{1,0:T(8,128)(2,1)S(1)} %get-tuple-element.15, bf16[16,8192]{1,0:T(8,128)(2,1)S(1)} %get-tuple-element.14), kind=kLoop, calls=%fused_computation.8 | loop fusion | flops 1048576 | bytes 1048576 | tf_op jit(solution)/shard_map/broadcast_in_dim | solution.py:311
  36.8 1.5 %assemble.1 = f32[256,2048]{1,0:T(8,128)} custom-call(bf16[32,2048]{1,0:T(8,128)(2,1)S(1)} %sum.1.refs_0_.refs_2_, bf16[32,2048]{1,0:T(8,128)(2,1)S(1)} %collective-permute-done.4.refs_1_, bf16[32,2048]{1,0:T(8,128)(2,1)S(1)} %collective-permute-done.5.refs_2_, bf16[32,2048]{1,0:T(8,128)(2,1)S(1)} %collective-permute-done.6.refs_3_, ...), custom_call_target="tpu_custom_call" | custom-call | tf_op jit(solution)/shard_map/assemble/pallas_call | solution.py:211
  (19 shorter events, 0.0 us)
Async XLA Ops:
  1.7 10.7 %collective-permute-start.11 = (bf16[16,8192]{1,0:T(8,128)(2,1)S(1)}, bf16[16,8192]{1,0:T(8,128)(2,1)S(1)}, u32[]{:S(2)}, u32[]{:S(2)}) collective-permute-start(bf16[16,8192]{1,0:T(8,128)(2,1)S(1)} %get-tuple-element.16.refs_1_), channel_id=1, source_target_pairs={{0,1},{4,5},{8,9},{12,13},{16,17},{20,21},{24,25},{28,29},{1,0},{5... | collective-permute-start | bytes 786440 | tf_op jit(solution)/shard_map/ppermute | solution.py:242
  4.8 13.4 %collective-permute-start.14 = (bf16[16,8192]{1,0:T(8,128)(2,1)S(1)}, bf16[16,8192]{1,0:T(8,128)(2,1)S(1)}, u32[]{:S(2)}, u32[]{:S(2)}) collective-permute-start(bf16[16,8192]{1,0:T(8,128)(2,1)S(1)} %get-tuple-element.17.refs_1_), channel_id=1, source_target_pairs={{0,1},{4,5},{8,9},{12,13},{16,17},{20,21},{24,25},{28,29},{1,0},{5... | collective-permute-start | bytes 786440 | tf_op jit(solution)/shard_map/ppermute | solution.py:242
  4.9 7.6 %copy-start.2 = (bf16[1,32,8192]{2,1,0:T(8,128)(2,1)S(1)}, bf16[1,32,8192]{2,1,0:T(8,128)(2,1)}, u32[]{:S(2)}) copy-start(bf16[1,32,8192]{2,1,0:T(8,128)(2,1)} %param.8) | copy-start | bytes 1572868
  4.9 8.2 %copy-start = (bf16[1,4,32,2048]{3,2,1,0:T(8,128)(2,1)S(1)}, bf16[1,4,32,2048]{3,2,1,0:T(8,128)(2,1)}, u32[]{:S(2)}) copy-start(bf16[1,4,32,2048]{3,2,1,0:T(8,128)(2,1)} %param.7) | copy-start | bytes 1572868
  12.4 2.2 %collective-permute-start = (bf16[128,2048]{1,0:T(8,128)(2,1)}, bf16[128,2048]{1,0:T(8,128)(2,1)S(1)}, u32[]{:S(2)}, u32[]{:S(2)}) collective-permute-start(bf16[128,2048]{1,0:T(8,128)(2,1)} %get-tuple-element.9), channel_id=1, source_target_pairs={{0,4},{4,0},{8,12},{12,8},{16,20},{20,16},{24,28},{28,24},{1,5},{5... | collective-permute-start | bytes 1572872 | tf_op jit(solution)/shard_map/ppermute | solution.py:173
  12.5 12.2 %collective-permute-start.12 = (bf16[16,8192]{1,0:T(8,128)(2,1)S(1)}, bf16[16,8192]{1,0:T(8,128)(2,1)S(1)}, u32[]{:S(2)}, u32[]{:S(2)}) collective-permute-start(bf16[16,8192]{1,0:T(8,128)(2,1)S(1)} %fusion), channel_id=1, source_target_pairs={{0,4},{4,0},{8,12},{12,8},{16,20},{20,16},{24,28},{28,24},{1,2},{5... | collective-permute-start | bytes 786440 | tf_op jit(solution)/shard_map/ppermute | solution.py:242
  13.1 0.8 %copy-start.1 = (bf16[2,128,128]{2,1,0:T(8,128)(2,1)S(1)}, bf16[2,128,128]{2,1,0:T(8,128)(2,1)}, u32[]{:S(2)}) copy-start(bf16[2,128,128]{2,1,0:T(8,128)(2,1)} %get-tuple-element.8.refs_0_) | copy-start | bytes 196612
  14.6 6.7 %collective-permute-start.1 = (bf16[32,2048]{1,0:T(8,128)(2,1)S(1)}, bf16[32,2048]{1,0:T(8,128)(2,1)S(1)}, u32[]{:S(2)}, u32[]{:S(2)}) collective-permute-start(bf16[32,2048]{1,0:T(8,128)(2,1)S(1)} %get-tuple-element.11), channel_id=1, source_target_pairs={{0,8},{4,12},{8,0},{12,4},{16,24},{20,28},{24,16},{28,20},{1,9},{5... | collective-permute-start | bytes 393224 | tf_op jit(solution)/shard_map/ppermute | solution.py:173
  16.6 8.1 %collective-permute-start.2 = (bf16[32,2048]{1,0:T(8,128)(2,1)S(1)}, bf16[32,2048]{1,0:T(8,128)(2,1)S(1)}, u32[]{:S(2)}, u32[]{:S(2)}) collective-permute-start(bf16[32,2048]{1,0:T(8,128)(2,1)S(1)} %get-tuple-element.12), channel_id=1, source_target_pairs={{0,16},{4,20},{8,24},{12,28},{16,0},{20,4},{24,8},{28,12},{1,17},{... | collective-permute-start | bytes 393224 | tf_op jit(solution)/shard_map/ppermute | solution.py:173
  18.1 6.5 %collective-permute-start.3 = (bf16[32,2048]{1,0:T(8,128)(2,1)S(1)}, bf16[32,2048]{1,0:T(8,128)(2,1)S(1)}, u32[]{:S(2)}, u32[]{:S(2)}) collective-permute-start(bf16[32,2048]{1,0:T(8,128)(2,1)S(1)} %get-tuple-element.13), channel_id=1, source_target_pairs={{0,24},{4,28},{8,16},{12,20},{16,8},{20,12},{24,0},{28,4},{1,25},{... | collective-permute-start | bytes 393224 | tf_op jit(solution)/shard_map/ppermute | solution.py:173
  18.3 11.7 %collective-permute-start.16 = (bf16[16,8192]{1,0:T(8,128)(2,1)S(1)}, bf16[16,8192]{1,0:T(8,128)(2,1)S(1)}, u32[]{:S(2)}, u32[]{:S(2)}) collective-permute-start(bf16[16,8192]{1,0:T(8,128)(2,1)S(1)} %add.52), channel_id=1, source_target_pairs={{0,2},{4,6},{8,10},{12,14},{16,18},{20,22},{24,26},{28,30},{1,5},{... | collective-permute-start | bytes 786440 | tf_op jit(solution)/shard_map/ppermute | solution.py:242
  21.3 9.5 %collective-permute-start.15 = (bf16[16,8192]{1,0:T(8,128)(2,1)S(1)}, bf16[16,8192]{1,0:T(8,128)(2,1)S(1)}, u32[]{:S(2)}, u32[]{:S(2)}) collective-permute-start(bf16[16,8192]{1,0:T(8,128)(2,1)S(1)} %add.52), channel_id=1, source_target_pairs={{0,4},{4,0},{8,12},{12,8},{16,20},{20,16},{24,28},{28,24},{1,2},{5... | collective-permute-start | bytes 786440 | tf_op jit(solution)/shard_map/ppermute | solution.py:242
  24.8 10.8 %collective-permute-start.13 = (bf16[16,8192]{1,0:T(8,128)(2,1)S(1)}, bf16[16,8192]{1,0:T(8,128)(2,1)S(1)}, u32[]{:S(2)}, u32[]{:S(2)}) collective-permute-start(bf16[16,8192]{1,0:T(8,128)(2,1)S(1)} %add.51), channel_id=1, source_target_pairs={{0,1},{4,5},{8,9},{12,13},{16,17},{20,21},{24,25},{28,29},{1,0},{5... | collective-permute-start | bytes 786440 | tf_op jit(solution)/shard_map/ppermute | solution.py:242
  27.3 6.9 %collective-permute-start.6 = (bf16[32,2048]{1,0:T(8,128)(2,1)S(1)}, bf16[32,2048]{1,0:T(8,128)(2,1)S(1)}, u32[]{:S(2)}, u32[]{:S(2)}) collective-permute-start(bf16[32,2048]{1,0:T(8,128)(2,1)S(1)} %sum.1.refs_0_.refs_2_), channel_id=1, source_target_pairs={{0,24},{4,28},{8,16},{12,20},{16,8},{20,12},{24,0},{28,4},{1,25},{... | collective-permute-start | bytes 393224 | tf_op jit(solution)/shard_map/ppermute | solution.py:173
  28.8 6.3 %collective-permute-start.5 = (bf16[32,2048]{1,0:T(8,128)(2,1)S(1)}, bf16[32,2048]{1,0:T(8,128)(2,1)S(1)}, u32[]{:S(2)}, u32[]{:S(2)}) collective-permute-start(bf16[32,2048]{1,0:T(8,128)(2,1)S(1)} %sum.1.refs_0_.refs_2_), channel_id=1, source_target_pairs={{0,16},{4,20},{8,24},{12,28},{16,0},{20,4},{24,8},{28,12},{1,17},{... | collective-permute-start | bytes 393224 | tf_op jit(solution)/shard_map/ppermute | solution.py:173
  30.0 5.3 %collective-permute-start.4 = (bf16[32,2048]{1,0:T(8,128)(2,1)S(1)}, bf16[32,2048]{1,0:T(8,128)(2,1)S(1)}, u32[]{:S(2)}, u32[]{:S(2)}) collective-permute-start(bf16[32,2048]{1,0:T(8,128)(2,1)S(1)} %sum.1.refs_0_.refs_2_), channel_id=1, source_target_pairs={{0,8},{4,12},{8,0},{12,4},{16,24},{20,28},{24,16},{28,20},{1,9},{5... | collective-permute-start | bytes 393224 | tf_op jit(solution)/shard_map/ppermute | solution.py:173
  30.8 6.0 %collective-permute-start.7 = (bf16[32,2048]{1,0:T(8,128)(2,1)S(1)}, bf16[32,2048]{1,0:T(8,128)(2,1)S(1)}, u32[]{:S(2)}, u32[]{:S(2)}) collective-permute-start(bf16[32,2048]{1,0:T(8,128)(2,1)S(1)} %sum.1.refs_0_.refs_2_), channel_id=1, source_target_pairs={{0,4},{4,0},{8,12},{12,8},{16,20},{20,16},{24,28},{28,24},{1,5},{5... | collective-permute-start | bytes 393224 | tf_op jit(solution)/shard_map/ppermute | solution.py:173
  34.2 2.5 %collective-permute-start.10 = (bf16[32,2048]{1,0:T(8,128)(2,1)S(1)}, bf16[32,2048]{1,0:T(8,128)(2,1)S(1)}, u32[]{:S(2)}, u32[]{:S(2)}) collective-permute-start(bf16[32,2048]{1,0:T(8,128)(2,1)S(1)} %collective-permute-done.6.refs_3_), channel_id=1, source_target_pairs={{0,4},{4,0},{8,12},{12,8},{16,20},{20,16},{24,28},{28,24},{1,5},{5... | collective-permute-start | bytes 393224 | tf_op jit(solution)/shard_map/ppermute | solution.py:173
  35.1 1.7 %collective-permute-start.9 = (bf16[32,2048]{1,0:T(8,128)(2,1)S(1)}, bf16[32,2048]{1,0:T(8,128)(2,1)S(1)}, u32[]{:S(2)}, u32[]{:S(2)}) collective-permute-start(bf16[32,2048]{1,0:T(8,128)(2,1)S(1)} %collective-permute-done.5.refs_2_), channel_id=1, source_target_pairs={{0,4},{4,0},{8,12},{12,8},{16,20},{20,16},{24,28},{28,24},{1,5},{5... | collective-permute-start | bytes 393224 | tf_op jit(solution)/shard_map/ppermute | solution.py:173
  35.4 1.4 %collective-permute-start.8 = (bf16[32,2048]{1,0:T(8,128)(2,1)S(1)}, bf16[32,2048]{1,0:T(8,128)(2,1)S(1)}, u32[]{:S(2)}, u32[]{:S(2)}) collective-permute-start(bf16[32,2048]{1,0:T(8,128)(2,1)S(1)} %collective-permute-done.4.refs_1_), channel_id=1, source_target_pairs={{0,4},{4,0},{8,12},{12,8},{16,20},{20,16},{24,28},{28,24},{1,5},{5... | collective-permute-start | bytes 393224 | tf_op jit(solution)/shard_map/ppermute | solution.py:173

commit v4 on v3

--- a/solution.py
+++ b/solution.py
@@ -190,16 +190,43 @@
     out[...] = total.astype(out.dtype)
 
 
-def assemble_kernel(axis, *refs):
-    *pieces, out = refs
-    chips = len(pieces) // 2
-    rows = pieces[0].shape[0]
-    device = lax.axis_index(axis)
-    for side in range(2):
-        core = lax.rem(device, 2) ^ side
-        for step in range(chips):
-            at = (core * chips + ((device // 2) ^ step)) * rows
-            out[pl.ds(pl.multiple_of(at, rows), rows), :] = pieces[side * chips + step][...].astype(out.dtype)
+def placed(blocks, at, out, before=None):
+    inside, anywhere = pl.BlockSpec(memory_space=pltpu.VMEM), pl.BlockSpec(memory_space=pl.ANY)
+    counts = [len(operands) for _, operands in blocks]
+    operands = [operand for _, group in blocks for operand in group]
+    earlier = [] if before is None else [before]
+    rows = [group[0].shape[0] for _, group in blocks]
+
+    def body(*refs):
+        ins, target = refs[:len(operands)], refs[len(operands) + len(earlier)]
+        scratch, sems = refs[len(operands) + len(earlier) + 1:-1], refs[-1]
+        copies, start = [], 0
+        for index, (make, _) in enumerate(blocks):
+            scratch[index][...] = make(*ins[start:start + counts[index]])
+            start += counts[index]
+            to = target.at[pl.ds(pl.multiple_of(at(index), rows[index]), rows[index])]
+            copies.append(pltpu.make_async_copy(scratch[index], to, sems.at[index]))
+            copies[-1].start()
+        for copy in copies:
+            copy.wait()
+
+    return pl.pallas_call(
+        body,
+        out_shape=out,
+        in_specs=[inside] * len(operands) + [anywhere] * len(earlier),
+        out_specs=anywhere,
+        scratch_shapes=[
+            *(pltpu.VMEM((count, *out.shape[1:]), out.dtype) for count in rows),
+            pltpu.SemaphoreType.DMA((len(blocks),)),
+        ],
+        input_output_aliases={len(operands): 0} if earlier else {},
+        compiler_params=pltpu.CompilerParams(vmem_limit_bytes=32 * 2**20),
+        name="place",
+    )(*operands, *earlier)
+
+
+def widened(ref):
+    return ref[...].astype(jnp.float32)
 
 
 def vmem_call(kernel, outs, name, *args, after=(), cost=None):
@@ -260,7 +287,6 @@
         kept, _ = compressed_parts(stash, kv, flora_seeds, plan, 1, "dp")
         return lax.psum(kept_part(kept, kv), "dp")[None], chain(branch, "pipe")[None]
 
-    mine = lax.axis_index("pipe")
     rows = branch.shape[0] // 2
     first, second = branch[:rows], branch[rows:]
     pairwise, middle, across = ((3, 2), (1, 0)), ((2, 1),), ((2, 0),)
@@ -293,21 +319,31 @@
     first_c = moved(first_1, pairwise)
     here = [done] + [exchanged(done, "dp", 2 * s) for s in range(1, chips)]
     there = [exchanged(value, "dp", 1) for value in here]
+    def at_rows(steps):
+        def at(index):
+            side, step = steps[index]
+            device = lax.axis_index("dp")
+            return ((lax.rem(device, 2) ^ side) * chips + ((device // 2) ^ step)) * piece[0]
+        return at
+
+    whole = jax.ShapeDtypeStruct((R, columns), jnp.float32)
+    early = [(side, step) for step in range(chips) for side in range(2)]
+    late = []
+    pieces = (here, there)
+    compressed = placed([(widened, [pieces[a][b]]) for a, b in early], at_rows(early), whole)
+    if late:
+        compressed = placed([(widened, [pieces[a][b]]) for a, b in late], at_rows(late), whole, compressed)
+
     def by_place(values):
         out = values[3]
         for place in range(3):
-            out = jnp.where(mine == place, values[place], out)
+            out = jnp.where(lax.axis_index("pipe") == place, values[place], out)
         return out
 
     running = jnp.concatenate([
         by_place([added(first_c, first), first_1, first_2, first]),
         by_place([added(added(second_d, second_a), second), added(second_b, second), second_2, second]),
     ])
-    compressed = vmem_call(
-        functools.partial(assemble_kernel, "dp"), jax.ShapeDtypeStruct((R, columns), jnp.float32),
-        "assemble", *here, *there, after=[],
-    )
-
     return compressed[None], running[None]
 
 

time: 38.5 us -> 38.4 us (level)
    pallas_call x6 -> x5, Pallas kernels: 2.07 us -> 0.59 us  [vmem_call(): pl.pallas_call(body, out_shape=outs, in_specs=[inside] * len(args) + [any...]
    pallas_call x0 -> x1, Pallas kernels: none -> 1.39 us  [placed(): pl.pallas_call(body, out_shape=out, in_specs=[inside] * len(operands) + [...]
where the time goes in v4:
time: 38.4 us; the launch traced here: 38.2 us
  starting transfers between devices  16.6 us (43%)
  Pallas kernels  9.47 us (25%)
  waiting for transfers between devices  8.21 us (21%)
  local copies, waits for them, and re-layouts  1.91 us (5%)
  other arithmetic  1.24 us (3%)
  between operations  0.73 us (2%)
    ppermute x6, starting transfers between devices, between_places(): return lax.ppermute(value, (other_axis, axis), pairs)  9.27 us
    ppermute x11, waiting for transfers between devices, exchanged(): return lax.ppermute(value, axis, [(i, i ^ distance) for i in range(size)])  8.19 us
    pallas_call x1, Pallas kernels, compressed_parts(): pl.pallas_call(functools.partial(compress_kernel, tile, groups, scale, ha...  7.49 us
    ppermute x11, starting transfers between devices, exchanged(): return lax.ppermute(value, axis, [(i, i ^ distance) for i in range(size)])  7.37 us
    pallas_call x1, Pallas kernels, placed(): pl.pallas_call(body, out_shape=out, in_specs=[inside] * len(operands) + [...  1.39 us
    slice x1, local copies, waits for them, and re-layouts, per_device(): first, second = (branch[:rows], branch[rows:])  1.07 us
    unnamed x6, local copies, waits for them, and re-layouts  0.85 us
    broadcast_in_dim x1, other arithmetic, per_device(): return (compressed[None], running[None])  0.83 us
  transfers between devices with their start and end apart: 17, of which 5 were waited for; matrix products, arithmetic and copies ran while one was open for 3% of the time, Pallas kernels for 21%

profile of v4, /device:TPU:0, one launch (start us, length us, event | category | flops | bytes accessed | tf_op | source)
XLA Modules:
  0.0 38.2 jit_solution(2992792112364268918)
XLA Ops:
  0.6 1.1 %slice_bitcast_fusion.1 = (bf16[16,8192]{1,0:T(8,128)(2,1)S(1)}, bf16[16,8192]{1,0:T(8,128)(2,1)S(1)}) fusion(bf16[1,32,8192]{2,1,0:T(8,128)(2,1)} %param.8), kind=kLoop, calls=%fused_computation.17 | loop fusion | bytes 1048576 | tf_op jit(solution)/shard_map/slice | solution.py:291
  1.7 3.1 %collective-permute-start.11 = (bf16[16,8192]{1,0:T(8,128)(2,1)S(1)}, bf16[16,8192]{1,0:T(8,128)(2,1)S(1)}, u32[]{:S(2)}, u32[]{:S(2)}) collective-permute-start(bf16[16,8192]{1,0:T(8,128)(2,1)S(1)} %get-tuple-element.16.refs_1_), channel_id=1, source_target_pairs={{0,1},{4,5},{8,9},{12,13},{16,17},{20,21},{24,25},{28,29},{1,0},{5... | collective-permute-start | bytes 786440 | tf_op jit(solution)/shard_map/ppermute | solution.py:269
  4.8 0.1 collective-permute-start.14
  4.9 7.5 %compress.1 = (bf16[2,128,128]{2,1,0:T(8,128)(2,1)}, bf16[128,2048]{1,0:T(8,128)(2,1)}) custom-call(s32[1,2]{1,0:T(1,128)} %seeds_hbm.1, s32[1,4]{1,0:T(1,128)} %plan_hbm.1, bf16[4,32,8192]{2,1,0:T(8,128)(2,1)} %bitcast.18, bf16[4,32,2048]{2,1,0:T(8,128)(2,1)} %bitcast.15, bf16[32,8192]{1,0:T(8,128)(2,1)} %constant.12.clone.digits_hbm), custom_call_target="tpu_custom_call" | custom-call | flops 8000000000 | bytes 28000000 | tf_op jit(solution)/shard_map/compress/pallas_call | solution.py:147
  12.4 0.1 collective-permute-start
  12.5 0.1 fusion
  12.5 0.5 %collective-permute-start.12 = (bf16[16,8192]{1,0:T(8,128)(2,1)S(1)}, bf16[16,8192]{1,0:T(8,128)(2,1)S(1)}, u32[]{:S(2)}, u32[]{:S(2)}) collective-permute-start(bf16[16,8192]{1,0:T(8,128)(2,1)S(1)} %fusion), channel_id=1, source_target_pairs={{0,4},{4,0},{8,12},{12,8},{16,20},{20,16},{24,28},{28,24},{1,2},{5... | collective-permute-start | bytes 786440 | tf_op jit(solution)/shard_map/ppermute | solution.py:269
  13.1 0.8 %copy-done.1 = bf16[2,128,128]{2,1,0:T(8,128)(2,1)S(1)} copy-done((bf16[2,128,128]{2,1,0:T(8,128)(2,1)S(1)}, bf16[2,128,128]{2,1,0:T(8,128)(2,1)}, u32[]{:S(2)}) %copy-start.1) | copy-done | bytes 65560
  13.9 0.3 keep.1.refs_0_.refs_2_
  14.2 0.3 collective-permute-done.refs_1_
  14.6 0.1 split.1
  14.6 1.9 %collective-permute-start.1 = (bf16[32,2048]{1,0:T(8,128)(2,1)S(1)}, bf16[32,2048]{1,0:T(8,128)(2,1)S(1)}, u32[]{:S(2)}, u32[]{:S(2)}) collective-permute-start(bf16[32,2048]{1,0:T(8,128)(2,1)S(1)} %get-tuple-element.11), channel_id=1, source_target_pairs={{0,8},{4,12},{8,0},{12,4},{16,24},{20,28},{24,16},{28,20},{1,9},{5... | collective-permute-start | bytes 393224 | tf_op jit(solution)/shard_map/ppermute | solution.py:173
  16.6 1.5 %collective-permute-start.2 = (bf16[32,2048]{1,0:T(8,128)(2,1)S(1)}, bf16[32,2048]{1,0:T(8,128)(2,1)S(1)}, u32[]{:S(2)}, u32[]{:S(2)}) collective-permute-start(bf16[32,2048]{1,0:T(8,128)(2,1)S(1)} %get-tuple-element.12), channel_id=1, source_target_pairs={{0,16},{4,20},{8,24},{12,28},{16,0},{20,4},{24,8},{28,12},{1,17},{... | collective-permute-start | bytes 393224 | tf_op jit(solution)/shard_map/ppermute | solution.py:173
  18.1 0.1 collective-permute-start.3
  18.2 0.1 add.52
  18.3 3.0 %collective-permute-start.16 = (bf16[16,8192]{1,0:T(8,128)(2,1)S(1)}, bf16[16,8192]{1,0:T(8,128)(2,1)S(1)}, u32[]{:S(2)}, u32[]{:S(2)}) collective-permute-start(bf16[16,8192]{1,0:T(8,128)(2,1)S(1)} %add.52), channel_id=1, source_target_pairs={{0,2},{4,6},{8,10},{12,14},{16,18},{20,22},{24,26},{28,30},{1,5},{... | collective-permute-start | bytes 786440 | tf_op jit(solution)/shard_map/ppermute | solution.py:269
  21.3 3.3 %collective-permute-done.2.refs_2_ = bf16[32,2048]{1,0:T(8,128)(2,1)S(1)} collective-permute-done((bf16[32,2048]{1,0:T(8,128)(2,1)S(1)}, bf16[32,2048]{1,0:T(8,128)(2,1)S(1)}, u32[]{:S(2)}, u32[]{:S(2)}) %collective-permute-start.2) | collective-permute-done | bytes 131104 | tf_op jit(solution)/shard_map/ppermute | solution.py:173
  24.6 0.1 sum.1.refs_0_.refs_2_
  24.7 0.0 collective-permute-done.12.refs_0_
  24.7 0.1 add.51
  24.8 2.5 %collective-permute-start.13 = (bf16[16,8192]{1,0:T(8,128)(2,1)S(1)}, bf16[16,8192]{1,0:T(8,128)(2,1)S(1)}, u32[]{:S(2)}, u32[]{:S(2)}) collective-permute-start(bf16[16,8192]{1,0:T(8,128)(2,1)S(1)} %add.51), channel_id=1, source_target_pairs={{0,1},{4,5},{8,9},{12,13},{16,17},{20,21},{24,25},{28,29},{1,0},{5... | collective-permute-start | bytes 786440 | tf_op jit(solution)/shard_map/ppermute | solution.py:269
  27.3 1.5 %collective-permute-start.9 = (bf16[32,2048]{1,0:T(8,128)(2,1)S(1)}, bf16[32,2048]{1,0:T(8,128)(2,1)S(1)}, u32[]{:S(2)}, u32[]{:S(2)}) collective-permute-start(bf16[32,2048]{1,0:T(8,128)(2,1)S(1)} %sum.1.refs_0_.refs_2_), channel_id=1, source_target_pairs={{0,24},{4,28},{8,16},{12,20},{16,8},{20,12},{24,0},{28,4},{1,25},{... | collective-permute-start | bytes 393224 | tf_op jit(solution)/shard_map/ppermute | solution.py:173
  28.8 1.2 %collective-permute-start.7 = (bf16[32,2048]{1,0:T(8,128)(2,1)S(1)}, bf16[32,2048]{1,0:T(8,128)(2,1)S(1)}, u32[]{:S(2)}, u32[]{:S(2)}) collective-permute-start(bf16[32,2048]{1,0:T(8,128)(2,1)S(1)} %sum.1.refs_0_.refs_2_), channel_id=1, source_target_pairs={{0,16},{4,20},{8,24},{12,28},{16,0},{20,4},{24,8},{28,12},{1,17},{... | collective-permute-start | bytes 393224 | tf_op jit(solution)/shard_map/ppermute | solution.py:173
  30.0 0.8 %collective-permute-start.5 = (bf16[32,2048]{1,0:T(8,128)(2,1)S(1)}, bf16[32,2048]{1,0:T(8,128)(2,1)S(1)}, u32[]{:S(2)}, u32[]{:S(2)}) collective-permute-start(bf16[32,2048]{1,0:T(8,128)(2,1)S(1)} %sum.1.refs_0_.refs_2_), channel_id=1, source_target_pairs={{0,8},{4,12},{8,0},{12,4},{16,24},{20,28},{24,16},{28,20},{1,9},{5... | collective-permute-start | bytes 393224 | tf_op jit(solution)/shard_map/ppermute | solution.py:173
  30.8 3.4 %collective-permute-done.9.refs_6_ = bf16[32,2048]{1,0:T(8,128)(2,1)S(1)} collective-permute-done((bf16[32,2048]{1,0:T(8,128)(2,1)S(1)}, bf16[32,2048]{1,0:T(8,128)(2,1)S(1)}, u32[]{:S(2)}, u32[]{:S(2)}) %collective-permute-start.9) | collective-permute-done | bytes 131104 | tf_op jit(solution)/shard_map/ppermute | solution.py:173
  34.2 0.8 %collective-permute-done.7.refs_4_ = bf16[32,2048]{1,0:T(8,128)(2,1)S(1)} collective-permute-done((bf16[32,2048]{1,0:T(8,128)(2,1)S(1)}, bf16[32,2048]{1,0:T(8,128)(2,1)S(1)}, u32[]{:S(2)}, u32[]{:S(2)}) %collective-permute-start.7) | collective-permute-done | bytes 131104 | tf_op jit(solution)/shard_map/ppermute | solution.py:173
  35.1 0.0 collective-permute-start.8
  35.1 0.3 collective-permute-done.5.refs_2_
  35.4 0.2 collective-permute-start.6
  35.6 0.3 fusion.7
  35.9 0.8 %maximum_bitcast_fusion = bf16[1,32,8192]{2,1,0:T(8,128)(2,1)} fusion(bf16[16,8192]{1,0:T(8,128)(2,1)S(1)} %get-tuple-element.15, bf16[16,8192]{1,0:T(8,128)(2,1)S(1)} %get-tuple-element.14), kind=kLoop, calls=%fused_computation.8 | loop fusion | flops 1048576 | bytes 1048576 | tf_op jit(solution)/shard_map/broadcast_in_dim | solution.py:347
  36.8 1.4 %place.1 = f32[256,2048]{1,0:T(8,128)} custom-call(bf16[32,2048]{1,0:T(8,128)(2,1)S(1)} %sum.1.refs_0_.refs_2_, bf16[32,2048]{1,0:T(8,128)(2,1)S(1)} %collective-permute-done.4.refs_1_, bf16[32,2048]{1,0:T(8,128)(2,1)S(1)} %collective-permute-done.5.refs_2_, bf16[32,2048]{1,0:T(8,128)(2,1)S(1)} %collective-permute-done.6.refs_3_, ...), custom_call_target="tpu_custom_call" | custom-call | tf_op jit(solution)/shard_map/place/pallas_call | solution.py:213
  (19 shorter events, 0.0 us)
Async XLA Ops:
  1.7 10.7 %collective-permute-start.11 = (bf16[16,8192]{1,0:T(8,128)(2,1)S(1)}, bf16[16,8192]{1,0:T(8,128)(2,1)S(1)}, u32[]{:S(2)}, u32[]{:S(2)}) collective-permute-start(bf16[16,8192]{1,0:T(8,128)(2,1)S(1)} %get-tuple-element.16.refs_1_), channel_id=1, source_target_pairs={{0,1},{4,5},{8,9},{12,13},{16,17},{20,21},{24,25},{28,29},{1,0},{5... | collective-permute-start | bytes 786440 | tf_op jit(solution)/shard_map/ppermute | solution.py:269
  4.8 13.4 %collective-permute-start.14 = (bf16[16,8192]{1,0:T(8,128)(2,1)S(1)}, bf16[16,8192]{1,0:T(8,128)(2,1)S(1)}, u32[]{:S(2)}, u32[]{:S(2)}) collective-permute-start(bf16[16,8192]{1,0:T(8,128)(2,1)S(1)} %get-tuple-element.17.refs_1_), channel_id=1, source_target_pairs={{0,1},{4,5},{8,9},{12,13},{16,17},{20,21},{24,25},{28,29},{1,0},{5... | collective-permute-start | bytes 786440 | tf_op jit(solution)/shard_map/ppermute | solution.py:269
  4.9 7.6 %copy-start.2 = (bf16[1,32,8192]{2,1,0:T(8,128)(2,1)S(1)}, bf16[1,32,8192]{2,1,0:T(8,128)(2,1)}, u32[]{:S(2)}) copy-start(bf16[1,32,8192]{2,1,0:T(8,128)(2,1)} %param.8) | copy-start | bytes 1572868
  4.9 8.2 %copy-start = (bf16[1,4,32,2048]{3,2,1,0:T(8,128)(2,1)S(1)}, bf16[1,4,32,2048]{3,2,1,0:T(8,128)(2,1)}, u32[]{:S(2)}) copy-start(bf16[1,4,32,2048]{3,2,1,0:T(8,128)(2,1)} %param.7) | copy-start | bytes 1572868
  12.4 2.2 %collective-permute-start = (bf16[128,2048]{1,0:T(8,128)(2,1)}, bf16[128,2048]{1,0:T(8,128)(2,1)S(1)}, u32[]{:S(2)}, u32[]{:S(2)}) collective-permute-start(bf16[128,2048]{1,0:T(8,128)(2,1)} %get-tuple-element.9), channel_id=1, source_target_pairs={{0,4},{4,0},{8,12},{12,8},{16,20},{20,16},{24,28},{28,24},{1,5},{5... | collective-permute-start | bytes 1572872 | tf_op jit(solution)/shard_map/ppermute | solution.py:173
  12.5 12.2 %collective-permute-start.12 = (bf16[16,8192]{1,0:T(8,128)(2,1)S(1)}, bf16[16,8192]{1,0:T(8,128)(2,1)S(1)}, u32[]{:S(2)}, u32[]{:S(2)}) collective-permute-start(bf16[16,8192]{1,0:T(8,128)(2,1)S(1)} %fusion), channel_id=1, source_target_pairs={{0,4},{4,0},{8,12},{12,8},{16,20},{20,16},{24,28},{28,24},{1,2},{5... | collective-permute-start | bytes 786440 | tf_op jit(solution)/shard_map/ppermute | solution.py:269
  13.1 0.8 %copy-start.1 = (bf16[2,128,128]{2,1,0:T(8,128)(2,1)S(1)}, bf16[2,128,128]{2,1,0:T(8,128)(2,1)}, u32[]{:S(2)}) copy-start(bf16[2,128,128]{2,1,0:T(8,128)(2,1)} %get-tuple-element.8.refs_0_) | copy-start | bytes 196612
  14.6 6.7 %collective-permute-start.1 = (bf16[32,2048]{1,0:T(8,128)(2,1)S(1)}, bf16[32,2048]{1,0:T(8,128)(2,1)S(1)}, u32[]{:S(2)}, u32[]{:S(2)}) collective-permute-start(bf16[32,2048]{1,0:T(8,128)(2,1)S(1)} %get-tuple-element.11), channel_id=1, source_target_pairs={{0,8},{4,12},{8,0},{12,4},{16,24},{20,28},{24,16},{28,20},{1,9},{5... | collective-permute-start | bytes 393224 | tf_op jit(solution)/shard_map/ppermute | solution.py:173
  16.6 8.1 %collective-permute-start.2 = (bf16[32,2048]{1,0:T(8,128)(2,1)S(1)}, bf16[32,2048]{1,0:T(8,128)(2,1)S(1)}, u32[]{:S(2)}, u32[]{:S(2)}) collective-permute-start(bf16[32,2048]{1,0:T(8,128)(2,1)S(1)} %get-tuple-element.12), channel_id=1, source_target_pairs={{0,16},{4,20},{8,24},{12,28},{16,0},{20,4},{24,8},{28,12},{1,17},{... | collective-permute-start | bytes 393224 | tf_op jit(solution)/shard_map/ppermute | solution.py:173
  18.1 6.5 %collective-permute-start.3 = (bf16[32,2048]{1,0:T(8,128)(2,1)S(1)}, bf16[32,2048]{1,0:T(8,128)(2,1)S(1)}, u32[]{:S(2)}, u32[]{:S(2)}) collective-permute-start(bf16[32,2048]{1,0:T(8,128)(2,1)S(1)} %get-tuple-element.13), channel_id=1, source_target_pairs={{0,24},{4,28},{8,16},{12,20},{16,8},{20,12},{24,0},{28,4},{1,25},{... | collective-permute-start | bytes 393224 | tf_op jit(solution)/shard_map/ppermute | solution.py:173
  18.3 11.7 %collective-permute-start.16 = (bf16[16,8192]{1,0:T(8,128)(2,1)S(1)}, bf16[16,8192]{1,0:T(8,128)(2,1)S(1)}, u32[]{:S(2)}, u32[]{:S(2)}) collective-permute-start(bf16[16,8192]{1,0:T(8,128)(2,1)S(1)} %add.52), channel_id=1, source_target_pairs={{0,2},{4,6},{8,10},{12,14},{16,18},{20,22},{24,26},{28,30},{1,5},{... | collective-permute-start | bytes 786440 | tf_op jit(solution)/shard_map/ppermute | solution.py:269
  21.3 9.5 %collective-permute-start.15 = (bf16[16,8192]{1,0:T(8,128)(2,1)S(1)}, bf16[16,8192]{1,0:T(8,128)(2,1)S(1)}, u32[]{:S(2)}, u32[]{:S(2)}) collective-permute-start(bf16[16,8192]{1,0:T(8,128)(2,1)S(1)} %add.52), channel_id=1, source_target_pairs={{0,4},{4,0},{8,12},{12,8},{16,20},{20,16},{24,28},{28,24},{1,2},{5... | collective-permute-start | bytes 786440 | tf_op jit(solution)/shard_map/ppermute | solution.py:269
  24.8 10.8 %collective-permute-start.13 = (bf16[16,8192]{1,0:T(8,128)(2,1)S(1)}, bf16[16,8192]{1,0:T(8,128)(2,1)S(1)}, u32[]{:S(2)}, u32[]{:S(2)}) collective-permute-start(bf16[16,8192]{1,0:T(8,128)(2,1)S(1)} %add.51), channel_id=1, source_target_pairs={{0,1},{4,5},{8,9},{12,13},{16,17},{20,21},{24,25},{28,29},{1,0},{5... | collective-permute-start | bytes 786440 | tf_op jit(solution)/shard_map/ppermute | solution.py:269
  27.3 6.9 %collective-permute-start.9 = (bf16[32,2048]{1,0:T(8,128)(2,1)S(1)}, bf16[32,2048]{1,0:T(8,128)(2,1)S(1)}, u32[]{:S(2)}, u32[]{:S(2)}) collective-permute-start(bf16[32,2048]{1,0:T(8,128)(2,1)S(1)} %sum.1.refs_0_.refs_2_), channel_id=1, source_target_pairs={{0,24},{4,28},{8,16},{12,20},{16,8},{20,12},{24,0},{28,4},{1,25},{... | collective-permute-start | bytes 393224 | tf_op jit(solution)/shard_map/ppermute | solution.py:173
  28.8 6.3 %collective-permute-start.7 = (bf16[32,2048]{1,0:T(8,128)(2,1)S(1)}, bf16[32,2048]{1,0:T(8,128)(2,1)S(1)}, u32[]{:S(2)}, u32[]{:S(2)}) collective-permute-start(bf16[32,2048]{1,0:T(8,128)(2,1)S(1)} %sum.1.refs_0_.refs_2_), channel_id=1, source_target_pairs={{0,16},{4,20},{8,24},{12,28},{16,0},{20,4},{24,8},{28,12},{1,17},{... | collective-permute-start | bytes 393224 | tf_op jit(solution)/shard_map/ppermute | solution.py:173
  30.0 5.3 %collective-permute-start.5 = (bf16[32,2048]{1,0:T(8,128)(2,1)S(1)}, bf16[32,2048]{1,0:T(8,128)(2,1)S(1)}, u32[]{:S(2)}, u32[]{:S(2)}) collective-permute-start(bf16[32,2048]{1,0:T(8,128)(2,1)S(1)} %sum.1.refs_0_.refs_2_), channel_id=1, source_target_pairs={{0,8},{4,12},{8,0},{12,4},{16,24},{20,28},{24,16},{28,20},{1,9},{5... | collective-permute-start | bytes 393224 | tf_op jit(solution)/shard_map/ppermute | solution.py:173
  30.8 6.0 %collective-permute-start.4 = (bf16[32,2048]{1,0:T(8,128)(2,1)S(1)}, bf16[32,2048]{1,0:T(8,128)(2,1)S(1)}, u32[]{:S(2)}, u32[]{:S(2)}) collective-permute-start(bf16[32,2048]{1,0:T(8,128)(2,1)S(1)} %sum.1.refs_0_.refs_2_), channel_id=1, source_target_pairs={{0,4},{4,0},{8,12},{12,8},{16,20},{20,16},{24,28},{28,24},{1,5},{5... | collective-permute-start | bytes 393224 | tf_op jit(solution)/shard_map/ppermute | solution.py:173
  34.2 2.5 %collective-permute-start.10 = (bf16[32,2048]{1,0:T(8,128)(2,1)S(1)}, bf16[32,2048]{1,0:T(8,128)(2,1)S(1)}, u32[]{:S(2)}, u32[]{:S(2)}) collective-permute-start(bf16[32,2048]{1,0:T(8,128)(2,1)S(1)} %collective-permute-done.9.refs_6_), channel_id=1, source_target_pairs={{0,4},{4,0},{8,12},{12,8},{16,20},{20,16},{24,28},{28,24},{1,5},{5... | collective-permute-start | bytes 393224 | tf_op jit(solution)/shard_map/ppermute | solution.py:173
  35.1 1.7 %collective-permute-start.8 = (bf16[32,2048]{1,0:T(8,128)(2,1)S(1)}, bf16[32,2048]{1,0:T(8,128)(2,1)S(1)}, u32[]{:S(2)}, u32[]{:S(2)}) collective-permute-start(bf16[32,2048]{1,0:T(8,128)(2,1)S(1)} %collective-permute-done.7.refs_4_), channel_id=1, source_target_pairs={{0,4},{4,0},{8,12},{12,8},{16,20},{20,16},{24,28},{28,24},{1,5},{5... | collective-permute-start | bytes 393224 | tf_op jit(solution)/shard_map/ppermute | solution.py:173
  35.4 1.4 %collective-permute-start.6 = (bf16[32,2048]{1,0:T(8,128)(2,1)S(1)}, bf16[32,2048]{1,0:T(8,128)(2,1)S(1)}, u32[]{:S(2)}, u32[]{:S(2)}) collective-permute-start(bf16[32,2048]{1,0:T(8,128)(2,1)S(1)} %collective-permute-done.5.refs_2_), channel_id=1, source_target_pairs={{0,4},{4,0},{8,12},{12,8},{16,20},{20,16},{24,28},{28,24},{1,5},{5... | collective-permute-start | bytes 393224 | tf_op jit(solution)/shard_map/ppermute | solution.py:173
